TPU v7x, 128 devices: a whole 4x4x4 slice. The times are simulated.
128 devices in a mesh: seq: 8 (over z_hi, x), tensor: 16 (over z_lo, y, core).
Axes of the slice: x: 4, y: 4, z: 4 (z_hi: 2, z_lo: 2; z = z_hi * 2 + z_lo), core: 2. Of those that a mesh axis runs over, the one named last changes fastest.
Arguments:
- inputs: bfloat16 [3072, 4096], P('seq', 'tensor'), may hold values from -6 to 6
- w_gate: bfloat16 [4096, 14336], P(None, 'tensor'), may hold values from -0.125 to 0.125
- w_up: bfloat16 [4096, 14336], P(None, 'tensor'), may hold values from -0.125 to 0.125
- w_down: bfloat16 [14336, 4096], P('tensor'), may hold values from -0.046875 to 0.046875
- cotangents: float32 [4, 3072, 4096], P(None, 'seq', 'tensor'), may hold values from -3 to 3
- prefix_widths: int32 [4], replicated, may hold values from 128 to 14336, as said below
- block_rank: int32 [112], P('tensor'), may hold values from 0 to 111, each once
Outputs:
- input_grads: bfloat16 [3072, 4096], P('seq', 'tensor')
- grad_gate: bfloat16 [4096, 14336], P('seq', 'tensor')
- grad_up: bfloat16 [4096, 14336], P('seq', 'tensor')
- grad_down: bfloat16 [14336, 4096], P('tensor', 'seq')
Inputs may be any that keep to these rules, and one draw needn't show every extreme that they name: prefix_widths[0] = 14336; the widths do not increase with g and are multiples of 128. `block_rank`: each number of 0 to 111 appears once.
All inputs are finite; a program needn't handle non-finite values.
Results may differ from a plain program's by a relative error of at most 0.025.
Values may be sent and summed in bfloat16 or wider, within the bound.
A program may use at most 192 MiB of HBM per device.

v0:
```python
import jax
import jax.numpy as jnp
from jax import lax
from jax.sharding import PartitionSpec as P

BLOCK = 128


def on_device(inputs, w_gate, w_up, w_down, cotangents, prefix_widths, block_rank):
    rows = lax.all_gather(inputs, "tensor", axis=1, tiled=True)
    tok = rows.shape[0]
    width = rows.shape[1]
    local_units = w_gate.shape[1]
    local_blocks = local_units // BLOCK
    whole = lax.all_gather(cotangents.astype(jnp.bfloat16), "tensor", axis=2, tiled=True).astype(
        cotangents.dtype
    )
    level_sums = jnp.cumsum(whole, axis=0).astype(jnp.bfloat16)
    gate = jnp.dot(rows, w_gate, preferred_element_type=jnp.float32)
    up = jnp.dot(rows, w_up, preferred_element_type=jnp.float32)
    sigma = jax.nn.sigmoid(gate)
    active = gate * sigma
    hidden = (active * up).astype(jnp.bfloat16)
    levels = jnp.sum(
        (block_rank[:, None] * BLOCK < prefix_widths[None, :]).astype(jnp.int32), axis=1
    )
    selected_width = jnp.take(level_sums, levels - 1, axis=0)
    down_weight_blocks = w_down.reshape(local_blocks, BLOCK, width)
    hidden_grad = jnp.einsum(
        "gmo,gio->mgi", selected_width, down_weight_blocks, preferred_element_type=jnp.float32
    ).reshape(tok, local_units)
    hidden_triple = hidden.reshape(tok, local_blocks, BLOCK)
    down_part = jnp.einsum(
        "qcs,cqw->csw", hidden_triple, selected_width, preferred_element_type=jnp.float32
    ).reshape(local_units, width)
    grad_down = lax.psum_scatter(
        down_part.astype(jnp.bfloat16), "seq", scatter_dimension=1, tiled=True
    )
    gate_grad = (hidden_grad * up * sigma * (1.0 + gate * (1.0 - sigma))).astype(jnp.bfloat16)
    up_grad = (hidden_grad * active).astype(jnp.bfloat16)
    first = lax.dot_general(
        w_gate, gate_grad, (((1,), (1,)), ((), ())), preferred_element_type=jnp.float32
    )
    latter_part = lax.dot_general(
        w_up, up_grad, (((1,), (1,)), ((), ())), preferred_element_type=jnp.float32
    )
    input_rows = lax.psum_scatter(
        (first + latter_part).astype(jnp.bfloat16), "tensor", scatter_dimension=0, tiled=True
    ).astype(jnp.float32)
    input_grads = input_rows.T.astype(jnp.bfloat16)
    first = lax.dot_general(
        rows, gate_grad, (((0,), (0,)), ((), ())), preferred_element_type=jnp.float32
    )
    latter_part = lax.dot_general(
        rows, up_grad, (((0,), (0,)), ((), ())), preferred_element_type=jnp.float32
    )
    paired = lax.psum_scatter(
        jnp.concatenate([first, latter_part], axis=1).astype(jnp.bfloat16),
        "seq",
        scatter_dimension=0,
        tiled=True,
    ).astype(jnp.float32)
    grad_gate = paired[:, :local_units].astype(jnp.bfloat16)
    grad_up = paired[:, local_units:].astype(jnp.bfloat16)
    return (input_grads, grad_gate, grad_up, grad_down)


def solution(mesh):
    placed = (
        P("seq", "tensor"),
        P(None, "tensor"),
        P(None, "tensor"),
        P("tensor", None),
        P(None, "seq", "tensor"),
        P(),
        P("tensor"),
    )
    return jax.shard_map(
        on_device,
        mesh=mesh,
        in_specs=placed,
        out_specs=(P("seq", "tensor"), P("seq", "tensor"), P("seq", "tensor"), P("tensor", "seq")),
        check_vma=False,
    )
```

profile of v0, /device:TPU:4, one launch (start us, length us, event | category | flops | bytes accessed | tf_op | source)
XLA Modules:
  0.0 569.8 jit_solution(5987291231529521627)
XLA Ops:
  7.2 0.0 all-gather.5.cloned.1.call-start
  7.2 0.7 all-gather.5.cloned.1.call-update
  7.9 0.0 all-gather.3.cloned.1.call-start
  7.9 2.4 convert_element_type.43
  10.3 0.0 reduce-scatter.6.cloned.1.call-start
  10.4 0.7 broadcast_multiply_fusion
  11.0 0.7 convert_reduce_fusion
  11.8 41.3 %all-gather.5.cloned.1.call-done = bf16[384,4096]{1,0:T(8,128)(2,1)} async-done(((bf16[384,256]{1,0:T(8,128)(2,1)}), bf16[384,4096]{1,0:T(8,128)(2,1)}) %all-gather.5.cloned.1.call-update) | async-done | bytes 3145744 | tf_op jit(solution)/shard_map/all_gather | solution.py:10
  53.1 8.6 %fusion.15 = f32[384,896]{1,0:T(8,128)} fusion(bf16[384,4096]{1,0:T(8,128)(2,1)} %all-gather.5.cloned.1.call-done, bf16[4096,896]{1,0:T(8,128)(2,1)} %param.8), kind=kOutput, calls=%fused_computation.31 | convolution fusion | flops 2818572288 | bytes 11862016 | tf_op jit(solution)/shard_map/dot_general | solution.py:19
  61.6 73.3 %all-gather.3.cloned.1.call-done = bf16[4,384,4096]{2,1,0:T(8,128)(2,1)} async-done(((bf16[4,384,256]{2,1,0:T(8,128)(2,1)}), bf16[4,384,4096]{2,1,0:T(8,128)(2,1)}) %all-gather.3.cloned.1.call-update) | async-done | bytes 12582928 | tf_op jit(solution)/shard_map/all_gather | solution.py:15
  135.0 10.4 %fusion.2 = bf16[4,384,4096]{2,1,0:T(8,128)(2,1)} fusion(bf16[4,384,4096]{2,1,0:T(8,128)(2,1)} %all-gather.3.cloned.1.call-done), kind=kOutput, calls=%fused_computation.6 | output fusion | flops 31457280 | bytes 25165824 | tf_op jit(solution)/shard_map/jit(cumsum)/reduce_window_sum | solution.py:18
  145.4 10.7 %fusion.13 = (bf16[4,384,2048]{2,1,0:T(8,128)(2,1)}, bf16[4,384,2048]{2,1,0:T(8,128)(2,1)}) fusion(bf16[4,384,4096]{2,1,0:T(8,128)(2,1)} %fusion.2), kind=kLoop, calls=%fused_computation.29 | loop fusion | bytes 25165824 | tf_op jit(solution)/shard_map/jit(_take)/gather | solution.py:27
  156.1 8.7 %gather_fusion = bf16[7,384,2048]{2,1,0:T(8,128)(2,1)} fusion(bf16[4,384,2048]{2,1,0:T(8,128)(2,1)} %get-tuple-element.16, s32[1024]{0:T(1024)S(1)} %pad_clamp_fusion), kind=kCustom, calls=%fused_computation | custom fusion | bytes 22020124 | tf_op jit(solution)/shard_map/jit(_take)/gather | solution.py:27
  164.8 8.7 %gather_fusion.1 = bf16[7,384,2048]{2,1,0:T(8,128)(2,1)} fusion(bf16[4,384,2048]{2,1,0:T(8,128)(2,1)} %get-tuple-element.17, s32[1024]{0:T(1024)S(1)} %pad_clamp_fusion), kind=kCustom, calls=%fused_computation.1 | custom fusion | bytes 22020124 | tf_op jit(solution)/shard_map/jit(_take)/gather | solution.py:27
  173.5 12.7 %fusion.7 = f32[7,384,128]{1,2,0:T(8,128)S(1)} fusion(bf16[7,128,4096]{2,1,0:T(8,128)(2,1)} %bitcast.36, bf16[7,384,2048]{2,1,0:T(8,128)(2,1)} %gather_fusion.1, bf16[7,384,2048]{2,1,0:T(8,128)(2,1)} %gather_fusion, pred[7]{0:T(512)(128)(4,1)S(1)} %compare_and_fusion), kind=kOutput, calls=%fused_computation.17 | convolution fusion | flops 2873622528 | bytes 30736392 | tf_op jit(solution)/shard_map/gmo,gio->mgi/dot_general | solution.py:29
  186.2 0.4 copy.21
  186.7 8.2 %multiply_convert_fusion = (bf16[384,896]{1,0:T(8,128)(2,1)S(1)}, bf16[384,896]{1,0:T(8,128)(2,1)S(1)}, bf16[384,896]{1,0:T(8,128)(2,1)S(1)}) fusion(f32[384,896]{1,0:T(8,128)} %fusion.15, f32[384,896]{1,0:T(8,128)S(1)} %copy.21, bf16[384,4096]{1,0:T(8,128)(2,1)} %all-gather.5.cloned.1.call-done, bf16[4096,896]{1,0:T(8,128)(2,1)} %param.9), kind=kOutput, calls=%fused_computation.12 | convolution fusion | flops 2823733248 | bytes 15302656 | tf_op jit(solution)/shard_map/dot_general | solution.py:20
  194.9 4.3 convert_bitcast_fusion
  199.2 4.2 convert_bitcast_fusion.1
  203.4 13.1 %pad_maximum_fusion = bf16[4096,1792]{0,1:T(8,128)(2,1)} fusion(bf16[4096,896]{0,1:T(8,128)(2,1)S(1)} %convert_bitcast_fusion, bf16[4096,896]{0,1:T(8,128)(2,1)S(1)} %convert_bitcast_fusion.1), kind=kLoop, calls=%fused_computation.5 | loop fusion | flops 29360128 | bytes 29360128 | tf_op jit(solution)/shard_map/concatenate | solution.py:58
  216.6 0.0 reduce-scatter.4.cloned.1.call-start
  216.6 5.8 %fusion.16 = f32[384,4096]{1,0:T(8,128)S(1)} fusion(bf16[384,896]{1,0:T(8,128)(2,1)S(1)} %get-tuple-element.19, bf16[4096,896]{1,0:T(8,128)(2,1)} %param.8), kind=kOutput, calls=%fused_computation.32 | convolution fusion | flops 2818572288 | bytes 14319616 | tf_op jit(solution)/shard_map/dot_general | solution.py:41
  222.4 9.6 %fusion.5 = bf16[4096,384]{0,1:T(8,128)(2,1)} fusion(f32[384,4096]{1,0:T(8,128)S(1)} %fusion.16, bf16[384,896]{1,0:T(8,128)(2,1)S(1)} %get-tuple-element.20, bf16[4096,896]{1,0:T(8,128)(2,1)} %param.9), kind=kOutput, calls=%fused_computation.11 | convolution fusion | flops 2821718016 | bytes 17465344 | tf_op jit(solution)/shard_map/dot_general | solution.py:44
  232.0 0.0 reduce-scatter.8.cloned.1.call-start
  232.1 0.4 copy.23
  232.4 15.6 %convolution_convert_fusion = bf16[7,128,4096]{2,1,0:T(8,128)(2,1)} fusion(bf16[384,7,128]{0,2,1:T(8,128)(2,1)S(1)} %bitcast.35, bf16[7,384,2048]{2,1,0:T(8,128)(2,1)} %gather_fusion.1, bf16[7,384,2048]{2,1,0:T(8,128)(2,1)} %gather_fusion, pred[7]{0:T(512)(128)(4,1)S(1)} %compare_and_fusion), kind=kOutput, calls=%fused_computation.9 | convolution fusion | flops 2877292544 | bytes 30048264 | tf_op jit(solution)/shard_map/qcs,cqw->csw/dot_general | solution.py:33
  248.1 137.8 %reduce-scatter.6.cloned.1.call-done = bf16[512,1792]{0,1:T(8,128)(2,1)} async-done(((bf16[4096,1792]{0,1:T(8,128)(2,1)}), bf16[512,1792]{0,1:T(8,128)(2,1)}) %reduce-scatter.6.cloned.1.call-update) | async-done | bytes 1835024 | tf_op jit(solution)/shard_map/reduce_scatter | solution.py:57
  385.9 1.6 fusion.14
  387.4 1.3 copy.25
  388.7 1.3 copy.24
  390.0 63.2 %reduce-scatter.4.cloned.1.call-done = bf16[256,384]{0,1:T(8,128)(2,1)} async-done(((bf16[4096,384]{0,1:T(8,128)(2,1)}), bf16[256,384]{0,1:T(8,128)(2,1)}) %reduce-scatter.4.cloned.1.call-update) | async-done | bytes 196624 | tf_op jit(solution)/shard_map/reduce_scatter | solution.py:47
  453.2 110.1 %reduce-scatter.8.cloned.1.call-done = bf16[896,512]{1,0:T(8,128)(2,1)} async-done(((bf16[896,4096]{1,0:T(8,128)(2,1)}), bf16[896,512]{1,0:T(8,128)(2,1)}) %reduce-scatter.8.cloned.1.call-update) | async-done | bytes 917520 | tf_op jit(solution)/shard_map/reduce_scatter | solution.py:36
  (9 shorter events, 0.1 us)
Async XLA Ops:
  7.2 45.9 %all-gather.5.cloned.1.call-start = ((), (), s32[]{:S(2)}) async-start(), calls=%async_computation.4 | async-start | bytes 3342336 | tf_op jit(solution)/shard_map/all_gather | solution.py:10
  7.9 127.1 %all-gather.3.cloned.1.call-start = ((), (), s32[]{:S(2)}) async-start(), calls=%async_computation.3 | async-start | bytes 13369344 | tf_op jit(solution)/shard_map/all_gather | solution.py:15
  10.3 375.5 %reduce-scatter.6.cloned.1.call-start = ((), (), s32[]{:S(2)}) async-start(), calls=%async_computation.6 | async-start | bytes 16515072 | tf_op jit(solution)/shard_map/reduce_scatter | solution.py:57
  186.7 8.2 %copy-start = (bf16[384,4096]{1,0:T(8,128)(2,1)S(1)}, bf16[384,4096]{1,0:T(8,128)(2,1)}, u32[]{:S(2)}) copy-start(bf16[384,4096]{1,0:T(8,128)(2,1)} %all-gather.5.cloned.1.call-done) | copy-start | bytes 9437188
  216.6 236.6 %reduce-scatter.4.cloned.1.call-start = ((), (), s32[]{:S(2)}) async-start(), calls=%async_computation.5 | async-start | bytes 3342336 | tf_op jit(solution)/shard_map/reduce_scatter | solution.py:47
  232.0 331.3 %reduce-scatter.8.cloned.1.call-start = ((), (), s32[]{:S(2)}) async-start(), calls=%async_computation.7 | async-start | bytes 8257536 | tf_op jit(solution)/shard_map/reduce_scatter | solution.py:36
Sparse Core Ops, SparseCore 0:
  9.6 43.4 all-gather.4
  55.3 79.6 all-gather.2
  216.7 169.1 reduce-scatter.5
  388.8 64.2 reduce-scatter.3
  458.0 105.2 reduce-scatter.7
where the time goes:
time: 572 us; the launch traced here: 570 us
  waiting for transfers between devices  426 us (74%)
  matrix products  69 us (12%)
  local copies, waits for them, and re-layouts  33.1 us (6%)
  other arithmetic  27.3 us (5%)
  between operations  13.8 us (2%)
    reduce_scatter x1, waiting for transfers between devices, on_device(): lax.psum_scatter(jnp.concatenate([first, latter_part], axis=1).astype(jnp...  138 us
    reduce_scatter x1, waiting for transfers between devices, on_device(): lax.psum_scatter(down_part.astype(jnp.bfloat16), 'seq', scatter_dimension...  110 us
    all_gather x1, waiting for transfers between devices, on_device(): lax.all_gather(cotangents.astype(jnp.bfloat16), 'tensor', axis=2, tiled=T...  73.3 us
    reduce_scatter x1, waiting for transfers between devices, on_device(): lax.psum_scatter((first + latter_part).astype(jnp.bfloat16), 'tensor', sc...  63.2 us
    all_gather x1, waiting for transfers between devices, on_device(): rows = lax.all_gather(inputs, 'tensor', axis=1, tiled=True)  41.3 us
    gather x3, local copies, waits for them, and re-layouts, on_device(): selected_width = jnp.take(level_sums, levels - 1, axis=0)  28.1 us
    dot_general x1, matrix products, on_device(): jnp.einsum('qcs,cqw->csw', hidden_triple, selected_width, preferred_eleme...  15.6 us
    concatenate x1, other arithmetic, on_device(): jnp.concatenate([first, latter_part], axis=1).astype(jnp.bfloat16)  13.1 us
  transfers between devices with their start and end apart: 5, of which 5 were waited for; matrix products, arithmetic and copies ran while one was open for 8% of the time, Pallas kernels for 0%

commit v1 on v0

v1 whole, which is shorter than its diff:
```python
import functools

import jax
import jax.numpy as jnp
from jax import lax
from jax.experimental import pallas as pl
from jax.experimental.pallas import tpu as pltpu
from jax.sharding import PartitionSpec as P

BLOCK = 128
LEVELS = 4
MESH = pl.DeviceIdType.MESH
COPIES = 128
F32 = jnp.float32
BF16 = jnp.bfloat16
NT = (((1,), (1,)), ((), ()))
ORDER = ((0, 0), (1, 0), (0, 3), (0, 1), (1, 3), (1, 1), (0, 2), (1, 2))


def dot(a, b):
    return jnp.dot(a, b, preferred_element_type=F32)


def dot_nt(a, b):
    return lax.dot_general(a, b, NT, preferred_element_type=F32)


def cols(start, size):
    return pl.ds(pl.multiple_of(start, 128), size)


def rows(start, size):
    return pl.ds(pl.multiple_of(start, 16), size)


def body(tok, width, units, *refs):
    widths, rank, xin, wg, wu, wd, cot, o_in, o_g, o_u, o_d = refs[:11]
    (X, wt, wdb, wrow, XTs, XT, G, D, R1, R2, R3, Ps, Pr, IrC, IrZ, IrY, A, B, HG, hT,
     ss, rs, ls, s1, r1, s2, r2) = refs[11 + 8:]
    LS = {place: refs[11 + i] for i, place in enumerate(ORDER)}
    nb = units // BLOCK
    half_t = tok // 2
    half_u = units // 2
    nchunk = 2 * units // 256

    s, t = lax.axis_index("seq"), lax.axis_index("tensor")
    x, zh = lax.rem(s, 4), s // 4
    zl, y, c = t // 8, lax.rem(t // 2, 4), lax.rem(t, 2)
    at_x = lambda k: (zh * 4 + lax.rem(x + k, 4), t)
    at_y = lambda k: (s, zl * 8 + lax.rem(y + k, 4) * 2 + c)
    C = (s, t + 1 - 2 * c)
    Z1 = (s, t + 8 - 16 * zl)
    Z2 = ((1 - zh) * 4 + x, t)
    Xp, Xm, X2, Yp, Ym, Y2 = at_x(1), at_x(3), at_x(2), at_y(1), at_y(3), at_y(2)

    started = []
    local = []

    def send(src, dst, dev):
        i = len(started)
        cp = pltpu.make_async_remote_copy(
            src_ref=src, dst_ref=dst, send_sem=ss.at[i], recv_sem=rs.at[i],
            device_id=dev, device_id_type=MESH)
        cp.start()
        started.append(cp)
        return cp

    def load(src, dst):
        i = len(local)
        cp = pltpu.make_async_copy(src, dst, ls.at[i])
        cp.start()
        local.append(cp)
        return cp

    cot_loads = [load(cot.at[g], A.at[:, cols(256 * g, 256)]) for g in range(3)]
    cot_loads.append(load(cot.at[3], B.at[:, cols(0, 256)]))
    own_x = load(xin, X.at[:, cols(t * 256, 256)])

    def tile_loads(b, slot):
        return (
            pltpu.make_async_copy(wg.at[:, cols(b * BLOCK, BLOCK)], wt.at[slot, :, cols(0, BLOCK)],
                                  ls.at[16 + 2 * slot]),
            pltpu.make_async_copy(wu.at[:, cols(b * BLOCK, BLOCK)], wt.at[slot, :, cols(BLOCK, BLOCK)],
                                  ls.at[17 + 2 * slot]),
        )

    for slot in range(2):
        for cp in tile_loads(slot, slot):
            cp.start()

    def feature_slice(place):
        return (zl + place[0] - 2 * zl * place[0]) * 4 + lax.rem(y + place[1], 4)

    def down_load(k):
        return pltpu.make_async_copy(wd.at[:, cols(feature_slice(ORDER[k]) * 512, 512)],
                                     wdb.at[k % 2], ls.at[20 + k % 2])

    down_load(0).start()
    down_load(1).start()

    barrier = pltpu.get_barrier_semaphore()
    peers = (C, Z1, Z2, Xp, Xm, X2, Yp, Ym, Y2)
    for dev in peers:
        pl.semaphore_signal(barrier, inc=1, device_id=dev, device_id_type=MESH)
    pl.semaphore_wait(barrier, len(peers))

    def x_view(dz, dy, half):
        tt = (zl + dz - 2 * zl * dz) * 8 + lax.rem(y + dy, 4) * 2 + c
        if half is None:
            return X.at[:, cols(tt * 256, 256)]
        return X.at[pl.ds(half * half_t, half_t), cols(tt * 256, 256)]

    def ls_view(dz, dy, half):
        if half is None:
            return LS[(dz, dy)].at[c]
        return LS[(dz, dy)].at[c, pl.ds(half * 2, 2)]

    def x_pair(dz, dy, half, step):
        return x_view(dz, dy, half), x_view(dz, dy, half)

    def ls_pair(dz, dy, half, step):
        moved = {"C": (dz, dy), "Z": (1 - dz, dy), "P": (dz, (dy + 3) % 4), "M": (dz, (dy + 1) % 4)}[step]
        return ls_view(dz, dy, half), ls_view(moved[0], moved[1], half)

    where = {"C": C, "Z": Z1, "P": Yp, "M": Ym}

    def gather_send(pair, dz, dy, half, step, src=None):
        a, b = pair(dz, dy, half, step)
        return send(a if src is None else src, b, where[step])

    to_z = gather_send(x_pair, 0, 0, None, "Z", xin)
    to_p = {0: gather_send(x_pair, 0, 0, None, "P", xin)}
    to_m = {0: gather_send(x_pair, 0, 0, None, "M", xin)}
    to_c = [gather_send(x_pair, 0, 0, None, "C", xin)]

    for cp in cot_loads:
        cp.wait()
    total = A[:, 0:256]
    own = LS[(0, 0)]
    own[c, 0] = total.astype(BF16)
    for g in range(1, LEVELS):
        total = total + (A[:, 256 * g:256 * g + 256] if g < 3 else B[:, 0:256])
        own[c, g] = total.astype(BF16)

    to_z.wait_recv()
    to_p[1] = gather_send(x_pair, 1, 0, None, "P")
    to_m[1] = gather_send(x_pair, 1, 0, None, "M")
    to_c.append(gather_send(x_pair, 1, 0, None, "C"))
    l_to_z = gather_send(ls_pair, 0, 0, None, "Z")
    l_to_c = {(0, 0): gather_send(ls_pair, 0, 0, None, "C")}
    opp = {}
    for dz in range(2):
        to_p[dz].wait_recv()
        opp[dz, 0] = gather_send(x_pair, dz, 3, 0, "P")
        to_c.append(gather_send(x_pair, dz, 3, None, "C"))
        to_m[dz].wait_recv()
        opp[dz, 1] = gather_send(x_pair, dz, 1, 1, "M")
        to_c.append(gather_send(x_pair, dz, 1, None, "C"))
    l_to_p = {0: gather_send(ls_pair, 0, 0, None, "P")}
    l_to_m = {0: gather_send(ls_pair, 0, 0, None, "M")}
    for dz in range(2):
        opp[dz, 0].wait_recv()
        opp[dz, 1].wait_recv()
        to_c.append(gather_send(x_pair, dz, 2, None, "C"))
    own_x.wait()
    for cp in to_c:
        cp.wait_recv()

    x_sends = [to_z, *to_p.values(), *to_m.values(), *opp.values(), *to_c]

    def transposed(k):
        return jnp.transpose(X[:, cols((c * 4 + lax.rem(x + k, 4)) * 512, 512)])

    x_moves = []
    for k, dev in ((1, Xp), (3, Xm), (2, X2)):
        XTs[k - 1] = transposed(k)
        x_moves.append((4 - k, send(XTs.at[k - 1], XT.at[c, :, cols((4 - k) * tok, tok)], dev)))
    XT[c, :, 0:tok] = transposed(0)
    xt_c = [send(XT.at[c, :, cols(0, tok)], XT.at[c, :, cols(0, tok)], C)]

    def forward(b, _):
        slot = lax.rem(b, 2)
        for cp in tile_loads(b, slot):
            cp.wait()
        both = dot(X[...], wt[slot])

        @pl.when(b + 2 < nb)
        def _():
            for cp in tile_loads(b + 2, slot):
                cp.start()

        gate, up = both[:, :BLOCK], both[:, BLOCK:]
        sigma = jax.nn.sigmoid(gate)
        active = gate * sigma
        at = cols(b * BLOCK, BLOCK)
        A[:, at] = up * sigma * (1.0 + gate * (1.0 - sigma))
        B[:, at] = active
        hT[rows(b * BLOCK, BLOCK), :] = jnp.transpose((active * up).astype(BF16))
        return 0

    lax.fori_loop(0, nb, forward, 0)

    for k, cp in x_moves:
        cp.wait_recv()
        piece = XT.at[c, :, cols(k * tok, tok)]
        xt_c.append(send(piece, piece, C))

    def relation(place):
        return lax.rem(y + place[1] - x + 4, 4)

    def owner_z(place):
        return zl + place[0] - 2 * zl * place[0]

    def reduce_copy(place, kind):
        dz, dy = place
        zz = owner_z(place)
        if kind < 2:
            return pltpu.make_async_remote_copy(
                src_ref=D.at[dz, dy, pl.ds(kind * half_u, half_u)], dst_ref=R1.at[zz, kind],
                send_sem=s1.at[zz, kind], recv_sem=r1.at[zz, kind],
                device_id=Xp if kind == 0 else Xm, device_id_type=MESH)
        rel = relation(place)
        side = rel // 2
        h = 1 - side if kind == 2 else side
        span = rows(h * half_u, half_u)
        return pltpu.make_async_remote_copy(
            src_ref=D.at[dz, dy, span], dst_ref=R2.at[zz, side, span],
            send_sem=s2.at[zz, side, kind - 2], recv_sem=r2.at[zz, side, kind - 2],
            device_id=at_x(rel), device_id_type=MESH)

    def slice_work(k):
        place = ORDER[k]
        dz, dy = place
        src = LS[place]
        down_load(k).wait()

        def step(b, _):
            used = sum((rank[b] * BLOCK < widths[g]).astype(jnp.int32) for g in range(LEVELS))
            level = jnp.maximum(used - 1, 0)
            l0, l1 = src[0, level], src[1, level]
            at = rows(b * BLOCK, BLOCK)
            h = hT[at, :]
            D[dz, dy, at, 0:256] = dot(h, l0).astype(BF16)
            D[dz, dy, at, 256:512] = dot(h, l1).astype(BF16)
            part = dot_nt(l0, wdb[k % 2, at, 0:256]) + dot_nt(l1, wdb[k % 2, at, 256:512])
            lane = cols(b * BLOCK, BLOCK)
            HG[:, lane] = part if k == 0 else HG[:, lane] + part
            return 0

        lax.fori_loop(0, nb, step, 0)
        if k + 2 < len(ORDER):
            down_load(k + 2).start()
        rel = relation(place)

        @pl.when(rel == 2)
        def _():
            reduce_copy(place, 0).start()
            reduce_copy(place, 1).start()

        @pl.when(lax.rem(rel, 2) == 1)
        def _():
            reduce_copy(place, 2).start()

    def relay(k):
        place = ORDER[k]
        dz, dy = place
        rel = relation(place)
        zz = owner_z(place)
        side = rel // 2

        @pl.when(lax.rem(rel, 2) == 1)
        def _():
            pltpu.make_async_remote_copy(
                src_ref=D.at[dz, dy, pl.ds(0, half_u)], dst_ref=R1.at[zz, side],
                send_sem=s1.at[zz, side], recv_sem=r1.at[zz, side],
                device_id=Xp, device_id_type=MESH).wait_recv()
            span = rows(side * half_u, half_u)
            D[dz, dy, span, :] = (D[dz, dy, span, :].astype(F32) + R1[zz, side].astype(F32)).astype(BF16)
            reduce_copy(place, 3).start()

    l_to_z.wait_recv()
    l_to_p[1] = gather_send(ls_pair, 1, 0, None, "P")
    l_to_m[1] = gather_send(ls_pair, 1, 0, None, "M")
    l_to_c[1, 0] = gather_send(ls_pair, 1, 0, None, "C")
    l_to_c[0, 0].wait_recv()
    slice_work(0)
    l_to_c[1, 0].wait_recv()
    slice_work(1)
    l_opp = {}
    for dz in range(2):
        l_to_p[dz].wait_recv()
        l_opp[dz, 0] = gather_send(ls_pair, dz, 3, 0, "P")
        l_to_c[dz, 3] = gather_send(ls_pair, dz, 3, None, "C")
        l_to_m[dz].wait_recv()
        l_opp[dz, 1] = gather_send(ls_pair, dz, 1, 1, "M")
        l_to_c[dz, 1] = gather_send(ls_pair, dz, 1, None, "C")
        for i, dy in enumerate((3, 1)):
            l_to_c[dz, dy].wait_recv()
            slice_work(2 + 2 * dz + i)
    for dz in range(2):
        l_opp[dz, 0].wait_recv()
        l_opp[dz, 1].wait_recv()
        l_to_c[dz, 2] = gather_send(ls_pair, dz, 2, None, "C")
        l_to_c[dz, 2].wait_recv()
        slice_work(6 + dz)
    for k in range(len(ORDER)):
        relay(k)

    def grads(b, _):
        at = cols(b * BLOCK, BLOCK)
        hg = HG[:, at]
        G[0:tok, at] = (hg * A[:, at]).astype(BF16)
        G[0:tok, cols(units + b * BLOCK, BLOCK)] = (hg * B[:, at]).astype(BF16)
        return 0

    lax.fori_loop(0, nb, grads, 0)

    from_m, from_p, far = {}, {}, {}

    def g_own(j):
        at = cols(j * 256, 256)
        src = G.at[pl.ds(0, tok), at]
        from_m[j] = send(src, G.at[pl.ds(3 * tok, tok), at], Xp)
        from_p[j] = send(src, G.at[pl.ds(tok, tok), at], Xm)

    def g_forward(j):
        at = cols(j * 256, 256)
        from_m[j].wait_recv()
        far[j, 0] = send(G.at[pl.ds(3 * tok, half_t), at], G.at[pl.ds(2 * tok, half_t), at], Xp)
        from_p[j].wait_recv()
        far[j, 1] = send(G.at[pl.ds(tok + half_t, half_t), at],
                         G.at[pl.ds(2 * tok + half_t, half_t), at], Xm)

    p_sent = {}

    def p_other(j):
        far[j, 0].wait_recv()
        far[j, 1].wait_recv()
        at = cols(j * 256, 256)
        for h in range(2):
            Ps[j, pl.ds(256 * h, 256), :] = dot(XT[1 - zh, pl.ds(256 * h, 256), :], G[:, at]).astype(BF16)
        p_sent[j] = send(Ps.at[j], Pr.at[j], Z2)

    def p_own(j):
        p_sent[j].wait_recv()
        at = cols(j * 256, 256)
        for h in range(2):
            r = pl.ds(256 * h, 256)
            out = (dot(XT[zh, r, :], G[:, at]) + Pr[j, r, :].astype(F32)).astype(BF16)
            for i in range(2):
                lane = j * 256 + i * BLOCK
                target, lane = (o_g, lane) if lane < units else (o_u, lane - units)
                target[r, lane:lane + BLOCK] = out[:, i * BLOCK:(i + 1) * BLOCK]

    def row_loads(i, slot, core):
        at = rows((2 * i + core) * 256, 256)
        return (
            pltpu.make_async_copy(wg.at[at, :], wrow.at[slot, :, cols(0, units)], ls.at[16 + 2 * slot]),
            pltpu.make_async_copy(wu.at[at, :], wrow.at[slot, :, cols(units, units)], ls.at[17 + 2 * slot]),
        )

    def input_part(core, offset):
        def step(i, _):
            slot = lax.rem(i, 2)
            for cp in row_loads(i, slot, core):
                cp.wait()
            X[:, cols(offset + i * 256, 256)] = dot_nt(G[0:tok, :], wrow[slot]).astype(BF16)

            @pl.when(i + 2 < 8)
            def _():
                for cp in row_loads(i + 2, slot, core):
                    cp.start()
            return 0

        for slot in range(2):
            for cp in row_loads(slot, slot, core):
                cp.start()
        lax.fori_loop(0, 8, step, 0)

    g_own(0)
    g_own(1)
    for cp in x_sends:
        cp.wait_send()
    input_part(1 - c, 0)
    in_c = send(X.at[:, cols(0, 2048)], IrC.at[...], C)
    g_own(2)
    g_forward(0)
    input_part(c, 2048)
    g_own(3)
    g_forward(1)
    for cp in xt_c:
        cp.wait_recv()
    p_other(0)
    in_c.wait_recv()
    away = cols(2048 + (1 - zl) * 1024, 1024)
    X[:, away] = (X[:, away].astype(F32) + IrC[:, cols((1 - zl) * 1024, 1024)].astype(F32)).astype(BF16)
    in_z = send(X.at[:, away], IrZ.at[...], Z1)
    g_own(4)
    g_forward(2)
    p_other(1)
    p_own(0)

    def sum_x(zz):
        for side in range(2):
            for i in range(2):
                span = pl.ds(0, half_u)
                pltpu.make_async_remote_copy(
                    src_ref=D.at[0, 0, span], dst_ref=R2.at[zz, side, span],
                    send_sem=s2.at[zz, side, i], recv_sem=r2.at[zz, side, i],
                    device_id=Xp, device_id_type=MESH).wait_recv()
        dz = zl + zz - 2 * zl * zz
        dy = lax.rem(x - y + 4, 4)
        return dz, dy

    def down_away():
        zz = 1 - zh
        dz, dy = sum_x(zz)

        def step(b, _):
            at = rows(b * BLOCK, BLOCK)
            D[dz, dy, at, :] = (D[dz, dy, at, :].astype(F32) + R2[zz, 0, at, :].astype(F32)
                                + R2[zz, 1, at, :].astype(F32)).astype(BF16)
            return 0

        lax.fori_loop(0, nb, step, 0)
        return send(D.at[dz, dy], R3.at[...], Z2)

    def down_own(cp):
        zz = zh
        dz, dy = sum_x(zz)
        cp.wait_recv()

        def step(b, _):
            at = rows(b * BLOCK, BLOCK)
            o_d[at, :] = (D[dz, dy, at, :].astype(F32) + R2[zz, 0, at, :].astype(F32)
                          + R2[zz, 1, at, :].astype(F32) + R3[at, :].astype(F32)).astype(BF16)
            return 0

        lax.fori_loop(0, nb, step, 0)

    down_z = down_away()
    g_own(5)
    g_forward(3)
    p_other(2)
    p_own(1)
    in_z.wait_recv()
    kept = cols(2048 + zl * 1024, 1024)
    X[:, kept] = (X[:, kept].astype(F32) + IrC[:, cols(zl * 1024, 1024)].astype(F32)
                  + IrZ[...].astype(F32)).astype(BF16)
    in_y = []
    for k, dev in ((1, Yp), (3, Ym), (2, Y2)):
        src = X.at[:, cols(2048 + zl * 1024 + lax.rem(y + k, 4) * 256, 256)]
        in_y.append(send(src, IrY.at[k - 1], dev))
    g_own(6)
    g_forward(4)
    p_other(3)
    p_own(2)
    g_forward(5)
    p_other(4)
    p_own(3)
    for cp in in_y:
        cp.wait_recv()
    mine = X[:, cols(2048 + zl * 1024 + y * 256, 256)].astype(F32)
    for k in range(3):
        mine = mine + IrY[k].astype(F32)
    o_in[...] = mine.astype(BF16)
    g_forward(6)
    p_other(5)
    p_own(4)
    p_other(6)
    down_own(down_z)
    p_own(5)
    p_own(6)

    for cp in started:
        if not any(cp is other for other in x_sends):
            cp.wait_send()
    for place in ORDER:
        rel = relation(place)

        @pl.when(rel == 2)
        def _():
            reduce_copy(place, 0).wait_send()
            reduce_copy(place, 1).wait_send()

        @pl.when(lax.rem(rel, 2) == 1)
        def _():
            reduce_copy(place, 2).wait_send()
            reduce_copy(place, 3).wait_send()


def on_device(inputs, w_gate, w_up, w_down, cotangents, prefix_widths, block_rank):
    tok = inputs.shape[0]
    width, units = w_gate.shape
    anywhere = pl.BlockSpec(memory_space=pl.ANY)
    smem = pl.BlockSpec(memory_space=pltpu.SMEM)
    vmem = pl.BlockSpec(memory_space=pltpu.VMEM)
    share = width // 8
    V = pltpu.VMEM
    dma = pltpu.SemaphoreType.DMA
    scratch = [V((2, LEVELS, tok, 256), BF16) for _ in ORDER] + [
        V((tok, width), BF16),
        V((2, width, 256), BF16),
        V((2, units, 512), BF16),
        V((2, 256, 2 * units), BF16),
        V((3, 512, tok), BF16),
        V((2, 512, 4 * tok), BF16),
        V((4 * tok, 2 * units), BF16),
        V((2, 4, units, 512), BF16),
        V((2, 2, units // 2, 512), BF16),
        V((2, 2, units, 512), BF16),
        V((units, 512), BF16),
        V((7, 512, 256), BF16),
        V((7, 512, 256), BF16),
        V((tok, width // 2), BF16),
        V((tok, width // 4), BF16),
        V((3, tok, 256), BF16),
        V((tok, units), F32),
        V((tok, units), F32),
        V((tok, units), F32),
        V((units, tok), BF16),
        dma((COPIES,)),
        dma((COPIES,)),
        dma((24,)),
        dma((2, 2)),
        dma((2, 2)),
        dma((2, 2, 2)),
        dma((2, 2, 2)),
    ]
    return pl.pallas_call(
        functools.partial(body, tok, width, units),
        out_shape=(
            jax.ShapeDtypeStruct((tok, 256), BF16),
            jax.ShapeDtypeStruct((share, units), BF16),
            jax.ShapeDtypeStruct((share, units), BF16),
            jax.ShapeDtypeStruct((units, share), BF16),
        ),
        in_specs=[smem, smem] + [anywhere] * 5,
        out_specs=(vmem,) * 4,
        scratch_shapes=scratch,
        compiler_params=pltpu.CompilerParams(
            collective_id=0, has_side_effects=True, vmem_limit_bytes=64 * 2**20),
        name="swiglu_backward",
    )(prefix_widths, block_rank, inputs, w_gate, w_up, w_down, cotangents)


def solution(mesh):
    placed = (
        P("seq", "tensor"),
        P(None, "tensor"),
        P(None, "tensor"),
        P("tensor", None),
        P(None, "seq", "tensor"),
        P(),
        P("tensor"),
    )
    return jax.shard_map(
        on_device,
        mesh=mesh,
        in_specs=placed,
        out_specs=(P("seq", "tensor"), P("seq", "tensor"), P("seq", "tensor"), P("tensor", "seq")),
        check_vma=False,
    )
```

time: 572 us -> 232 us (0.41)
  waiting for transfers between devices: 426 us -> 0 us
  Pallas kernels: 0 us -> 222 us
  matrix products: 69 us -> 0 us
  other arithmetic: 27.3 us -> 0 us
  local copies, waits for them, and re-layouts: 33.1 us -> 8.12 us
  between operations: 13.8 us -> 0.64 us
    reduce_scatter x3 -> x0, waiting for transfers between devices: 311 us -> none  [the longest x1 138 us: on_device(): lax.psum_scatter(jnp.concatenate([first, latter_part], axis=1).astype(jnp...]
    pallas_call x0 -> x1, Pallas kernels: none -> 222 us  [on_device(): pl.pallas_call(functools.partial(body, tok, width, units), out_shape=(jax...]
    all_gather x2 -> x0, waiting for transfers between devices: 115 us -> none  [the longest x1 73.3 us: on_device(): lax.all_gather(cotangents.astype(jnp.bfloat16), 'tensor', axis=2, tiled=T...]
    dot_general x8 -> x0, matrix products: 69 us -> none  [the longest x1 15.6 us: on_device(): jnp.einsum('qcs,cqw->csw', hidden_triple, selected_width, preferred_eleme...]
    gather x3 -> x0, local copies, waits for them, and re-layouts: 28.1 us -> none  [on_device(): selected_width = jnp.take(level_sums, levels - 1, axis=0)]
    concatenate x1 -> x0, other arithmetic: 13.1 us -> none  [on_device(): jnp.concatenate([first, latter_part], axis=1).astype(jnp.bfloat16)]
    another operation x1 -> x0, other arithmetic: 10.4 us -> none  [on_device(): level_sums = jnp.cumsum(whole, axis=0).astype(jnp.bfloat16)]
  transfers between devices with their start and end apart: 5 -> 0, of which waited for: 5 -> 0; matrix products, arithmetic and copies ran while one was open for 8% -> 0% of each run, Pallas kernels for 0% -> 0%
where the time goes in v1:
time: 232 us; the launch traced here: 231 us
  Pallas kernels  222 us (96%)
  local copies, waits for them, and re-layouts  8.12 us (3%)
    pallas_call x1, Pallas kernels, on_device(): pl.pallas_call(functools.partial(body, tok, width, units), out_shape=(jax...  222 us
    unnamed x4, local copies, waits for them, and re-layouts  8.12 us

profile of v1, /device:TPU:4, one launch (start us, length us, event | category | flops | bytes accessed | tf_op | source)
XLA Modules:
  0.0 231.1 jit_solution(6884581385132897019)
XLA Ops:
  0.6 222.4 %swiglu_backward.1 = (bf16[384,256]{1,0:T(8,128)(2,1)}, bf16[512,896]{1,0:T(8,128)(2,1)}, bf16[512,896]{1,0:T(8,128)(2,1)}, bf16[896,512]{1,0:T(8,128)(2,1)}) custom-call(s32[4]{0:T(128)} %refs_0_.1, s32[7]{0:T(128)} %refs_1_.1, bf16[384,256]{1,0:T(8,128)(2,1)} %refs_2_.1, bf16[4096,896]{1,0:T(8,128)(2,1)} %refs_3_.1, bf16[4096,896]{1,0:T(8,128)(2,1)} %refs_4_.1, ...), custom_call_target="tpu_custom_call" | custom-call | tf_op jit(solution)/shard_map/swiglu_backward/pallas_call | solution.py:530
  223.0 1.6 copy.15
  224.6 2.2 copy.16
  226.8 2.2 copy.17
  229.0 2.2 copy.18

commit v2 on v1

--- a/solution.py
+++ b/solution.py
@@ -14,7 +14,7 @@
 F32 = jnp.float32
 BF16 = jnp.bfloat16
 NT = (((1,), (1,)), ((), ()))
-ORDER = ((0, 0), (1, 0), (0, 3), (0, 1), (1, 3), (1, 1), (0, 2), (1, 2))
+ORDER = ((0, 0), (1, 0), (0, 3), (0, 1), (0, 2), (1, 3), (1, 1), (1, 2))
 
 
 def dot(a, b):
@@ -39,7 +39,7 @@
      ss, rs, ls, s1, r1, s2, r2) = refs[11 + 8:]
     LS = {place: refs[11 + i] for i, place in enumerate(ORDER)}
     nb = units // BLOCK
-    half_t = tok // 2
+    half_t, quarter = tok // 2, tok // 4
     half_u = units // 2
     nchunk = 2 * units // 256
 
@@ -76,15 +76,20 @@
     cot_loads.append(load(cot.at[3], B.at[:, cols(0, 256)]))
     own_x = load(xin, X.at[:, cols(t * 256, 256)])
 
-    def tile_loads(b, slot):
+    half_w = width // 2
+
+    def tile_half(n):
+        h = n // nb
+        return zl + h - 2 * zl * h
+
+    def tile_loads(n, slot):
+        at, lane = rows(tile_half(n) * half_w, half_w), cols(lax.rem(n, nb) * BLOCK, BLOCK)
         return (
-            pltpu.make_async_copy(wg.at[:, cols(b * BLOCK, BLOCK)], wt.at[slot, :, cols(0, BLOCK)],
-                                  ls.at[16 + 2 * slot]),
-            pltpu.make_async_copy(wu.at[:, cols(b * BLOCK, BLOCK)], wt.at[slot, :, cols(BLOCK, BLOCK)],
-                                  ls.at[17 + 2 * slot]),
+            pltpu.make_async_copy(wg.at[at, lane], wt.at[slot, :, cols(0, BLOCK)], ls.at[8 + 2 * slot]),
+            pltpu.make_async_copy(wu.at[at, lane], wt.at[slot, :, cols(BLOCK, BLOCK)], ls.at[9 + 2 * slot]),
         )
 
-    for slot in range(2):
+    for slot in range(4):
         for cp in tile_loads(slot, slot):
             cp.start()
 
@@ -104,34 +109,82 @@
         pl.semaphore_signal(barrier, inc=1, device_id=dev, device_id_type=MESH)
     pl.semaphore_wait(barrier, len(peers))
 
-    def x_view(dz, dy, half):
-        tt = (zl + dz - 2 * zl * dz) * 8 + lax.rem(y + dy, 4) * 2 + c
-        if half is None:
-            return X.at[:, cols(tt * 256, 256)]
-        return X.at[pl.ds(half * half_t, half_t), cols(tt * 256, 256)]
-
-    def ls_view(dz, dy, half):
-        if half is None:
-            return LS[(dz, dy)].at[c]
-        return LS[(dz, dy)].at[c, pl.ds(half * 2, 2)]
-
-    def x_pair(dz, dy, half, step):
-        return x_view(dz, dy, half), x_view(dz, dy, half)
-
-    def ls_pair(dz, dy, half, step):
-        moved = {"C": (dz, dy), "Z": (1 - dz, dy), "P": (dz, (dy + 3) % 4), "M": (dz, (dy + 1) % 4)}[step]
-        return ls_view(dz, dy, half), ls_view(moved[0], moved[1], half)
-
-    where = {"C": C, "Z": Z1, "P": Yp, "M": Ym}
-
-    def gather_send(pair, dz, dy, half, step, src=None):
-        a, b = pair(dz, dy, half, step)
-        return send(a if src is None else src, b, where[step])
-
-    to_z = gather_send(x_pair, 0, 0, None, "Z", xin)
-    to_p = {0: gather_send(x_pair, 0, 0, None, "P", xin)}
-    to_m = {0: gather_send(x_pair, 0, 0, None, "M", xin)}
-    to_c = [gather_send(x_pair, 0, 0, None, "C", xin)]
+    def x_view(place, first, count):
+        tt = feature_slice(place) * 2 + c
+        return X.at[pl.ds(first * quarter, count * quarter), cols(tt * 256, 256)]
+
+    def x_pair(place, moved, first, count):
+        return x_view(place, first, count), x_view(place, first, count)
+
+    def ls_pair(place, moved, first, count):
+        levels = pl.ds(first, count)
+        return LS[place].at[c, levels], LS[moved].at[c, levels]
+
+    class Gather:
+        def __init__(self, pair, cut):
+            self.pair = pair
+            self.cut = cut
+            self.moves = {}
+
+        def send(self, step, place, first=0, count=4, src=None):
+            dz, dy = place
+            moved, dev = {"C": (place, C), "Z": ((1 - dz, dy), Z1), "P": ((dz, (dy + 3) % 4), Yp),
+                          "M": ((dz, (dy + 1) % 4), Ym)}[step]
+            mine, there = self.pair(place, moved, first, count)
+            self.moves[step, place] = send(mine if src is None else src, there, dev)
+
+        def got(self, step, place):
+            self.moves[step, place].wait_recv()
+
+        def late_z(self, place):
+            if self.cut < 4:
+                self.send("Z", place, self.cut, 4 - self.cut)
+
+        def got_late_z(self, place):
+            if self.cut < 4:
+                self.got("Z", place)
+
+        def along_z(self):
+            self.got("Z", (0, 0))
+            self.send("P", (1, 0), 0, self.cut)
+            self.send("M", (1, 0), 0, self.cut)
+            self.send("C", (1, 0))
+
+        def neighbours0(self):
+            self.got("P", (0, 0))
+            self.send("P", (0, 3), 0, 2)
+            self.late_z((0, 3))
+            self.send("C", (0, 3))
+            self.got("M", (0, 0))
+            self.send("M", (0, 1), 2, 2)
+            self.late_z((0, 1))
+            self.send("C", (0, 1))
+
+        def opposite0(self):
+            self.got("P", (0, 3))
+            self.got("M", (0, 1))
+            self.late_z((0, 2))
+            self.send("C", (0, 2))
+
+        def neighbours1(self):
+            self.got("P", (1, 0))
+            self.send("P", (1, 3), 0, self.cut // 2)
+            self.got("M", (1, 0))
+            self.send("M", (1, 1), self.cut // 2, self.cut // 2)
+            self.got_late_z((0, 3))
+            self.send("C", (1, 3))
+            self.got_late_z((0, 1))
+            self.send("C", (1, 1))
+
+        def opposite1(self):
+            self.got("P", (1, 3))
+            self.got("M", (1, 1))
+            self.got_late_z((0, 2))
+            self.send("C", (1, 2))
+
+    gx, gl = Gather(x_pair, 4), Gather(ls_pair, 2)
+    for step in "ZPMC":
+        gx.send(step, (0, 0), src=xin)
 
     for cp in cot_loads:
         cp.wait()
@@ -142,31 +195,55 @@
         total = total + (A[:, 256 * g:256 * g + 256] if g < 3 else B[:, 0:256])
         own[c, g] = total.astype(BF16)
 
-    to_z.wait_recv()
-    to_p[1] = gather_send(x_pair, 1, 0, None, "P")
-    to_m[1] = gather_send(x_pair, 1, 0, None, "M")
-    to_c.append(gather_send(x_pair, 1, 0, None, "C"))
-    l_to_z = gather_send(ls_pair, 0, 0, None, "Z")
-    l_to_c = {(0, 0): gather_send(ls_pair, 0, 0, None, "C")}
-    opp = {}
-    for dz in range(2):
-        to_p[dz].wait_recv()
-        opp[dz, 0] = gather_send(x_pair, dz, 3, 0, "P")
-        to_c.append(gather_send(x_pair, dz, 3, None, "C"))
-        to_m[dz].wait_recv()
-        opp[dz, 1] = gather_send(x_pair, dz, 1, 1, "M")
-        to_c.append(gather_send(x_pair, dz, 1, None, "C"))
-    l_to_p = {0: gather_send(ls_pair, 0, 0, None, "P")}
-    l_to_m = {0: gather_send(ls_pair, 0, 0, None, "M")}
-    for dz in range(2):
-        opp[dz, 0].wait_recv()
-        opp[dz, 1].wait_recv()
-        to_c.append(gather_send(x_pair, dz, 2, None, "C"))
+    gx.along_z()
+    gl.send("Z", (0, 0))
+    gl.send("C", (0, 0))
+    gx.neighbours0()
+    gx.opposite0()
+    gx.neighbours1()
+    gl.send("P", (0, 0))
+    gl.send("M", (0, 0))
     own_x.wait()
-    for cp in to_c:
-        cp.wait_recv()
-
-    x_sends = [to_z, *to_p.values(), *to_m.values(), *opp.values(), *to_c]
+    for dy in range(4):
+        gx.got("C", (0, dy))
+
+    def forward_part(n):
+        slot = lax.rem(n, 4)
+        for cp in tile_loads(n, slot):
+            cp.wait()
+        return dot(X[:, cols(tile_half(n) * half_w, half_w)], wt[slot])
+
+    def tile_next(n):
+        @pl.when(n + 4 < 2 * nb)
+        def _():
+            for cp in tile_loads(n + 4, lax.rem(n, 4)):
+                cp.start()
+
+    def forward_first(b, _):
+        both = forward_part(b)
+        tile_next(b)
+        at = cols(b * BLOCK, BLOCK)
+        A[:, at] = both[:, :BLOCK]
+        B[:, at] = both[:, BLOCK:]
+        return 0
+
+    def forward(b, _):
+        both = forward_part(b + nb)
+        tile_next(b + nb)
+        at = cols(b * BLOCK, BLOCK)
+        gate, up = both[:, :BLOCK] + A[:, at], both[:, BLOCK:] + B[:, at]
+        sigma = jax.nn.sigmoid(gate)
+        active = gate * sigma
+        A[:, at] = up * sigma * (1.0 + gate * (1.0 - sigma))
+        B[:, at] = active
+        hT[rows(b * BLOCK, BLOCK), :] = jnp.transpose((active * up).astype(BF16))
+        return 0
+
+    lax.fori_loop(0, nb, forward_first, 0)
+    gx.opposite1()
+    for dy in range(4):
+        gx.got("C", (1, dy))
+    x_sends = list(gx.moves.values())
 
     def transposed(k):
         return jnp.transpose(X[:, cols((c * 4 + lax.rem(x + k, 4)) * 512, 512)])
@@ -178,32 +255,7 @@
     XT[c, :, 0:tok] = transposed(0)
     xt_c = [send(XT.at[c, :, cols(0, tok)], XT.at[c, :, cols(0, tok)], C)]
 
-    def forward(b, _):
-        slot = lax.rem(b, 2)
-        for cp in tile_loads(b, slot):
-            cp.wait()
-        both = dot(X[...], wt[slot])
-
-        @pl.when(b + 2 < nb)
-        def _():
-            for cp in tile_loads(b + 2, slot):
-                cp.start()
-
-        gate, up = both[:, :BLOCK], both[:, BLOCK:]
-        sigma = jax.nn.sigmoid(gate)
-        active = gate * sigma
-        at = cols(b * BLOCK, BLOCK)
-        A[:, at] = up * sigma * (1.0 + gate * (1.0 - sigma))
-        B[:, at] = active
-        hT[rows(b * BLOCK, BLOCK), :] = jnp.transpose((active * up).astype(BF16))
-        return 0
-
     lax.fori_loop(0, nb, forward, 0)
-
-    for k, cp in x_moves:
-        cp.wait_recv()
-        piece = XT.at[c, :, cols(k * tok, tok)]
-        xt_c.append(send(piece, piece, C))
 
     def relation(place):
         return lax.rem(y + place[1] - x + 4, 4)
@@ -278,33 +330,36 @@
             D[dz, dy, span, :] = (D[dz, dy, span, :].astype(F32) + R1[zz, side].astype(F32)).astype(BF16)
             reduce_copy(place, 3).start()
 
-    l_to_z.wait_recv()
-    l_to_p[1] = gather_send(ls_pair, 1, 0, None, "P")
-    l_to_m[1] = gather_send(ls_pair, 1, 0, None, "M")
-    l_to_c[1, 0] = gather_send(ls_pair, 1, 0, None, "C")
-    l_to_c[0, 0].wait_recv()
+    gl.along_z()
+    gl.got("C", (0, 0))
     slice_work(0)
-    l_to_c[1, 0].wait_recv()
+    gl.neighbours0()
+    gl.got("C", (1, 0))
     slice_work(1)
-    l_opp = {}
-    for dz in range(2):
-        l_to_p[dz].wait_recv()
-        l_opp[dz, 0] = gather_send(ls_pair, dz, 3, 0, "P")
-        l_to_c[dz, 3] = gather_send(ls_pair, dz, 3, None, "C")
-        l_to_m[dz].wait_recv()
-        l_opp[dz, 1] = gather_send(ls_pair, dz, 1, 1, "M")
-        l_to_c[dz, 1] = gather_send(ls_pair, dz, 1, None, "C")
-        for i, dy in enumerate((3, 1)):
-            l_to_c[dz, dy].wait_recv()
-            slice_work(2 + 2 * dz + i)
-    for dz in range(2):
-        l_opp[dz, 0].wait_recv()
-        l_opp[dz, 1].wait_recv()
-        l_to_c[dz, 2] = gather_send(ls_pair, dz, 2, None, "C")
-        l_to_c[dz, 2].wait_recv()
-        slice_work(6 + dz)
-    for k in range(len(ORDER)):
-        relay(k)
+    gl.got("C", (0, 3))
+    slice_work(2)
+    gl.got("C", (0, 1))
+    slice_work(3)
+    gl.opposite0()
+    for k, cp in x_moves:
+        cp.wait_recv()
+        piece = XT.at[c, :, cols(k * tok, tok)]
+        xt_c.append(send(piece, piece, C))
+    relay(0)
+    gl.got("C", (0, 2))
+    slice_work(4)
+    gl.neighbours1()
+    relay(1)
+    gl.got("C", (1, 3))
+    slice_work(5)
+    gl.got("C", (1, 1))
+    slice_work(6)
+    gl.opposite1()
+    relay(2)
+    relay(3)
+    gl.got("C", (1, 2))
+    slice_work(7)
+    relay(4)
 
     def grads(b, _):
         at = cols(b * BLOCK, BLOCK)
@@ -377,29 +432,6 @@
                 cp.start()
         lax.fori_loop(0, 8, step, 0)
 
-    g_own(0)
-    g_own(1)
-    for cp in x_sends:
-        cp.wait_send()
-    input_part(1 - c, 0)
-    in_c = send(X.at[:, cols(0, 2048)], IrC.at[...], C)
-    g_own(2)
-    g_forward(0)
-    input_part(c, 2048)
-    g_own(3)
-    g_forward(1)
-    for cp in xt_c:
-        cp.wait_recv()
-    p_other(0)
-    in_c.wait_recv()
-    away = cols(2048 + (1 - zl) * 1024, 1024)
-    X[:, away] = (X[:, away].astype(F32) + IrC[:, cols((1 - zl) * 1024, 1024)].astype(F32)).astype(BF16)
-    in_z = send(X.at[:, away], IrZ.at[...], Z1)
-    g_own(4)
-    g_forward(2)
-    p_other(1)
-    p_own(0)
-
     def sum_x(zz):
         for side in range(2):
             for i in range(2):
@@ -408,27 +440,26 @@
                     src_ref=D.at[0, 0, span], dst_ref=R2.at[zz, side, span],
                     send_sem=s2.at[zz, side, i], recv_sem=r2.at[zz, side, i],
                     device_id=Xp, device_id_type=MESH).wait_recv()
-        dz = zl + zz - 2 * zl * zz
-        dy = lax.rem(x - y + 4, 4)
-        return dz, dy
-
-    def down_away():
+        return down_place(zz)
+
+    def down_place(zz):
+        return zl + zz - 2 * zl * zz, lax.rem(x - y + 4, 4)
+
+    down_z = []
+
+    def down_away(half):
         zz = 1 - zh
-        dz, dy = sum_x(zz)
-
-        def step(b, _):
-            at = rows(b * BLOCK, BLOCK)
-            D[dz, dy, at, :] = (D[dz, dy, at, :].astype(F32) + R2[zz, 0, at, :].astype(F32)
-                                + R2[zz, 1, at, :].astype(F32)).astype(BF16)
-            return 0
-
-        lax.fori_loop(0, nb, step, 0)
-        return send(D.at[dz, dy], R3.at[...], Z2)
-
-    def down_own(cp):
+        dz, dy = sum_x(zz) if half == 0 else down_place(zz)
+        at = pl.ds(half * half_u, half_u)
+        D[dz, dy, at, :] = (D[dz, dy, at, :].astype(F32) + R2[zz, 0, at, :].astype(F32)
+                            + R2[zz, 1, at, :].astype(F32)).astype(BF16)
+        down_z.append(send(D.at[dz, dy, at], R3.at[at], Z2))
+
+    def down_own():
         zz = zh
         dz, dy = sum_x(zz)
-        cp.wait_recv()
+        for cp in down_z:
+            cp.wait_recv()
 
         def step(b, _):
             at = rows(b * BLOCK, BLOCK)
@@ -438,37 +469,75 @@
 
         lax.fori_loop(0, nb, step, 0)
 
-    down_z = down_away()
+    in_y, in_z = [], []
+
+    def input_sum_cores():
+        in_c.wait_recv()
+        for i in range(8):
+            at = cols(2048 + 256 * i, 256)
+            X[:, at] = (X[:, at].astype(F32) + IrC[:, cols(256 * i, 256)].astype(F32)).astype(BF16)
+        for k, dev in ((1, Yp), (3, Ym), (2, Y2)):
+            for zz in range(2):
+                src = X.at[:, cols(2048 + zz * 1024 + lax.rem(y + k, 4) * 256, 256)]
+                in_y.append(send(src, IrY.at[k - 1, zz], dev))
+
+    def input_sum_y():
+        for cp in in_y:
+            cp.wait_recv()
+        for zz in range(2):
+            at = cols(2048 + zz * 1024 + y * 256, 256)
+            total = X[:, at].astype(F32)
+            for k in range(3):
+                total = total + IrY[k, zz].astype(F32)
+            X[:, at] = total.astype(BF16)
+        in_z.append(send(X.at[:, cols(2048 + (1 - zl) * 1024 + y * 256, 256)], IrZ.at[...], Z1))
+
+    def input_sum_z():
+        in_z[0].wait_recv()
+        o_in[...] = (X[:, cols(2048 + zl * 1024 + y * 256, 256)].astype(F32) + IrZ[...].astype(F32)).astype(BF16)
+
+    g_own(0)
+    g_own(1)
+    g_own(2)
+    for cp in x_sends:
+        cp.wait_send()
+    input_part(1 - c, 0)
+    in_c = send(X.at[:, cols(0, 2048)], IrC.at[...], C)
+    relay(5)
+    relay(6)
+    input_part(c, 2048)
+    relay(7)
+    for cp in xt_c:
+        cp.wait_recv()
+    input_sum_cores()
+    g_forward(0)
+    g_own(3)
+    g_forward(1)
+    g_own(4)
+    down_away(0)
+    down_away(1)
+    p_other(0)
+    g_forward(2)
     g_own(5)
+    p_other(1)
     g_forward(3)
+    g_own(6)
     p_other(2)
-    p_own(1)
-    in_z.wait_recv()
-    kept = cols(2048 + zl * 1024, 1024)
-    X[:, kept] = (X[:, kept].astype(F32) + IrC[:, cols(zl * 1024, 1024)].astype(F32)
-                  + IrZ[...].astype(F32)).astype(BF16)
-    in_y = []
-    for k, dev in ((1, Yp), (3, Ym), (2, Y2)):
-        src = X.at[:, cols(2048 + zl * 1024 + lax.rem(y + k, 4) * 256, 256)]
-        in_y.append(send(src, IrY.at[k - 1], dev))
-    g_own(6)
+    input_sum_y()
     g_forward(4)
     p_other(3)
-    p_own(2)
     g_forward(5)
+    p_own(0)
     p_other(4)
-    p_own(3)
-    for cp in in_y:
-        cp.wait_recv()
-    mine = X[:, cols(2048 + zl * 1024 + y * 256, 256)].astype(F32)
-    for k in range(3):
-        mine = mine + IrY[k].astype(F32)
-    o_in[...] = mine.astype(BF16)
+    p_own(1)
     g_forward(6)
     p_other(5)
+    p_own(2)
+    p_other(6)
+    input_sum_z()
+    p_own(3)
     p_own(4)
-    p_other(6)
-    down_own(down_z)
+    down_own()
     p_own(5)
     p_own(6)
 
@@ -487,6 +556,19 @@
         def _():
             reduce_copy(place, 2).wait_send()
             reduce_copy(place, 3).wait_send()
+
+
+def hand_out(*refs):
+    src, dst, held, sems = refs[:4], refs[4:8], refs[8:12], refs[12]
+    into = [pltpu.make_async_copy(src[i], held[i], sems.at[0, i]) for i in range(4)]
+    out = [pltpu.make_async_copy(held[i], dst[i], sems.at[1, i]) for i in range(4)]
+    for cp in into:
+        cp.start()
+    for i in range(4):
+        into[i].wait()
+        out[i].start()
+    for cp in out:
+        cp.wait()
 
 
 def on_device(inputs, w_gate, w_up, w_down, cotangents, prefix_widths, block_rank):
@@ -500,7 +582,7 @@
     dma = pltpu.SemaphoreType.DMA
     scratch = [V((2, LEVELS, tok, 256), BF16) for _ in ORDER] + [
         V((tok, width), BF16),
-        V((2, width, 256), BF16),
+        V((4, width // 2, 256), BF16),
         V((2, units, 512), BF16),
         V((2, 256, 2 * units), BF16),
         V((3, 512, tok), BF16),
@@ -513,8 +595,8 @@
         V((7, 512, 256), BF16),
         V((7, 512, 256), BF16),
         V((tok, width // 2), BF16),
-        V((tok, width // 4), BF16),
-        V((3, tok, 256), BF16),
+        V((tok, 256), BF16),
+        V((3, 2, tok, 256), BF16),
         V((tok, units), F32),
         V((tok, units), F32),
         V((tok, units), F32),
@@ -527,7 +609,7 @@
         dma((2, 2, 2)),
         dma((2, 2, 2)),
     ]
-    return pl.pallas_call(
+    results = pl.pallas_call(
         functools.partial(body, tok, width, units),
         out_shape=(
             jax.ShapeDtypeStruct((tok, 256), BF16),
@@ -542,6 +624,14 @@
             collective_id=0, has_side_effects=True, vmem_limit_bytes=64 * 2**20),
         name="swiglu_backward",
     )(prefix_widths, block_rank, inputs, w_gate, w_up, w_down, cotangents)
+    return pl.pallas_call(
+        hand_out,
+        out_shape=tuple(jax.ShapeDtypeStruct(r.shape, r.dtype) for r in results),
+        in_specs=[anywhere] * 4,
+        out_specs=(anywhere,) * 4,
+        scratch_shapes=[V(r.shape, r.dtype) for r in results] + [dma((2, 4))],
+        name="hand_out",
+    )(*results)
 
 
 def solution(mesh):

time: 232 us -> 198 us (0.85); the launches traced: 231 us -> 194 us
  Pallas kernels: 222 us -> 193 us
  local copies, waits for them, and re-layouts: 8.12 us -> 0 us
    pallas_call x1, Pallas kernels: 222 us -> 191 us  [on_device(): pl.pallas_call(functools.partial(body, tok, width, units), out_shape=(jax...]
    unnamed x4 -> x0, local copies, waits for them, and re-layouts: 8.12 us -> none
    pallas_call x0 -> x1, Pallas kernels: none -> 2.89 us  [on_device(): pl.pallas_call(hand_out, out_shape=tuple((jax.ShapeDtypeStruct(r.shape, r...]
where the time goes in v2:
time: 198 us; the launch traced here: 194 us
  Pallas kernels  193 us (97%)
    pallas_call x1, Pallas kernels, on_device(): pl.pallas_call(functools.partial(body, tok, width, units), out_shape=(jax...  191 us

profile of v2, /device:TPU:4, one launch (start us, length us, event | category | flops | bytes accessed | tf_op | source)
XLA Modules:
  0.0 194.3 jit_solution(9616958147399106297)
XLA Ops:
  0.6 190.6 %swiglu_backward.1 = (bf16[384,256]{1,0:T(8,128)(2,1)}, bf16[512,896]{1,0:T(8,128)(2,1)}, bf16[512,896]{1,0:T(8,128)(2,1)}, bf16[896,512]{1,0:T(8,128)(2,1)}) custom-call(s32[4]{0:T(128)} %refs_0_.1, s32[7]{0:T(128)} %refs_1_.1, bf16[384,256]{1,0:T(8,128)(2,1)} %refs_2_.1, bf16[4096,896]{1,0:T(8,128)(2,1)} %refs_3_.1, bf16[4096,896]{1,0:T(8,128)(2,1)} %refs_4_.1, ...), custom_call_target="tpu_custom_call" | custom-call | tf_op jit(solution)/shard_map/swiglu_backward/pallas_call | solution.py:612
  191.2 2.9 %hand_out.1 = (bf16[384,256]{1,0:T(8,128)(2,1)}, bf16[512,896]{1,0:T(8,128)(2,1)}, bf16[512,896]{1,0:T(8,128)(2,1)}, bf16[896,512]{1,0:T(8,128)(2,1)}) custom-call(bf16[384,256]{1,0:T(8,128)(2,1)} %get-tuple-element.8.refs_0_, bf16[512,896]{1,0:T(8,128)(2,1)} %get-tuple-element.9.refs_1_, bf16[512,896]{1,0:T(8,128)(2,1)} %get-tuple-element.10.refs_2_, ...), custom_call_target="tpu_custom_call" | custom-call | tf_op jit(solution)/shard_map/hand_out/pallas_call | solution.py:627

commit v3 on v2

--- a/solution.py
+++ b/solution.py
@@ -11,6 +11,7 @@
 LEVELS = 4
 MESH = pl.DeviceIdType.MESH
 COPIES = 128
+Z_BLOCKS = 4
 F32 = jnp.float32
 BF16 = jnp.bfloat16
 NT = (((1,), (1,)), ((), ()))
@@ -33,14 +34,14 @@
     return pl.ds(pl.multiple_of(start, 16), size)
 
 
-def body(tok, width, units, *refs):
-    widths, rank, xin, wg, wu, wd, cot, o_in, o_g, o_u, o_d = refs[:11]
+def body(tok, width, units, z_rows, *refs):
+    widths, rank, xin, wg, wu, wd, cot, to_in, to_g, to_u, to_d = refs[:11]
     (X, wt, wdb, wrow, XTs, XT, G, D, R1, R2, R3, Ps, Pr, IrC, IrZ, IrY, A, B, HG, hT,
-     ss, rs, ls, s1, r1, s2, r2) = refs[11 + 8:]
+     ss, rs, ls, s1, r1, s2, r2, RZ, R1A, R2A, s1a, r1a, s2a, r2a, sz, rz,
+     o_in, o_g, o_u, o_d, so) = refs[11 + 8:]
     LS = {place: refs[11 + i] for i, place in enumerate(ORDER)}
     nb = units // BLOCK
     half_t, quarter = tok // 2, tok // 4
-    half_u = units // 2
     nchunk = 2 * units // 256
 
     s, t = lax.axis_index("seq"), lax.axis_index("tensor")
@@ -81,6 +82,13 @@
     def tile_half(n):
         h = n // nb
         return zl + h - 2 * zl * h
+
+    stored = []
+
+    def store(held, out):
+        cp = pltpu.make_async_copy(held, out, so.at[len(stored)])
+        cp.start()
+        stored.append(cp)
 
     def tile_loads(n, slot):
         at, lane = rows(tile_half(n) * half_w, half_w), cols(lax.rem(n, nb) * BLOCK, BLOCK)
@@ -245,15 +253,41 @@
         gx.got("C", (1, dy))
     x_sends = list(gx.moves.values())
 
-    def transposed(k):
-        return jnp.transpose(X[:, cols((c * 4 + lax.rem(x + k, 4)) * 512, 512)])
-
+    def transposed(zz):
+        return jnp.transpose(X[:, cols((zz * 4 + x) * 512, 512)])
+
+    share = 512 // 8
+    mine = rows((zl * 4 + y) * share, share)
+    far_tokens = pl.ds(tok, 3 * tok)
     x_moves = []
     for k, dev in ((1, Xp), (3, Xm), (2, X2)):
-        XTs[k - 1] = transposed(k)
-        x_moves.append((4 - k, send(XTs.at[k - 1], XT.at[c, :, cols((4 - k) * tok, tok)], dev)))
-    XT[c, :, 0:tok] = transposed(0)
-    xt_c = [send(XT.at[c, :, cols(0, tok)], XT.at[c, :, cols(0, tok)], C)]
+        lanes = cols((c * 4 + lax.rem(x + k, 4)) * 512 + (zl * 2 + y // 2) * 128, 128)
+        block = jnp.transpose(X[:, lanes])
+        XTs[k - 1] = jnp.where(lax.rem(y, 2) == 0, block[:share], block[share:])
+        x_moves.append(send(XTs.at[k - 1], XT.at[c, mine, cols((4 - k) * tok, tok)], dev))
+    for zz in range(2):
+        XT[zz, :, 0:tok] = transposed(zz)
+    xt_moves = {}
+
+    def xt_along_z():
+        for cp in x_moves:
+            cp.wait_recv()
+        piece = XT.at[c, mine, far_tokens]
+        xt_moves["Z"] = send(piece, piece, Z1)
+
+    def xt_around_y():
+        xt_moves["Z"].wait_recv()
+        for k, dev in ((1, Yp), (3, Ym), (2, Y2)):
+            for h in range(2):
+                piece = XT.at[c, rows((h * 4 + y) * share, share), far_tokens]
+                xt_moves[k, h] = send(piece, piece, dev)
+
+    def xt_cores():
+        for k in (1, 3, 2):
+            for h in range(2):
+                xt_moves[k, h].wait_recv()
+        piece = XT.at[c, :, far_tokens]
+        xt_moves["C"] = send(piece, piece, C)
 
     lax.fori_loop(0, nb, forward, 0)
 
@@ -263,22 +297,111 @@
     def owner_z(place):
         return zl + place[0] - 2 * zl * place[0]
 
-    def reduce_copy(place, kind):
+    early = (0, z_rows // 2, R1A, R2A, s1a, r1a, s2a, r2a)
+    late = (z_rows, (units - z_rows) // 2, R1, R2, s1, r1, s2, r2)
+
+    def at_owner(ref, part, zz, *index):
+        return ref.at[index] if part is early else ref.at[(zz, *index)]
+
+    def reduce_copy(part, place, kind):
+        base, half, one, two, send1, recv1, send2, recv2 = part
         dz, dy = place
         zz = owner_z(place)
         if kind < 2:
             return pltpu.make_async_remote_copy(
-                src_ref=D.at[dz, dy, pl.ds(kind * half_u, half_u)], dst_ref=R1.at[zz, kind],
-                send_sem=s1.at[zz, kind], recv_sem=r1.at[zz, kind],
+                src_ref=D.at[dz, dy, pl.ds(base + kind * half, half)],
+                dst_ref=at_owner(one, part, zz, kind),
+                send_sem=at_owner(send1, part, zz, kind), recv_sem=at_owner(recv1, part, zz, kind),
                 device_id=Xp if kind == 0 else Xm, device_id_type=MESH)
         rel = relation(place)
         side = rel // 2
         h = 1 - side if kind == 2 else side
-        span = rows(h * half_u, half_u)
         return pltpu.make_async_remote_copy(
-            src_ref=D.at[dz, dy, span], dst_ref=R2.at[zz, side, span],
-            send_sem=s2.at[zz, side, kind - 2], recv_sem=r2.at[zz, side, kind - 2],
+            src_ref=D.at[dz, dy, rows(base + h * half, half)],
+            dst_ref=at_owner(two, part, zz, side, rows(h * half, half)),
+            send_sem=at_owner(send2, part, zz, side, kind - 2),
+            recv_sem=at_owner(recv2, part, zz, side, kind - 2),
             device_id=at_x(rel), device_id_type=MESH)
+
+    def reduce_first(part, place):
+        rel = relation(place)
+
+        @pl.when(rel == 2)
+        def _():
+            reduce_copy(part, place, 0).start()
+            reduce_copy(part, place, 1).start()
+
+        @pl.when(lax.rem(rel, 2) == 1)
+        def _():
+            reduce_copy(part, place, 2).start()
+
+    def reduce_relay(part, place):
+        base, half, one, two, send1, recv1, send2, recv2 = part
+        dz, dy = place
+        rel = relation(place)
+        zz = owner_z(place)
+        side = rel // 2
+
+        @pl.when(lax.rem(rel, 2) == 1)
+        def _():
+            pltpu.make_async_remote_copy(
+                src_ref=D.at[dz, dy, pl.ds(base, half)], dst_ref=at_owner(one, part, zz, side),
+                send_sem=at_owner(send1, part, zz, side), recv_sem=at_owner(recv1, part, zz, side),
+                device_id=Xp, device_id_type=MESH).wait_recv()
+            span = rows(base + side * half, half)
+            D[dz, dy, span, :] = (D[dz, dy, span, :].astype(F32)
+                                  + at_owner(one, part, zz, side)[...].astype(F32)).astype(BF16)
+            reduce_copy(part, place, 3).start()
+
+    def reduce_drain(part, place):
+        rel = relation(place)
+
+        @pl.when(rel == 2)
+        def _():
+            reduce_copy(part, place, 0).wait_send()
+            reduce_copy(part, place, 1).wait_send()
+
+        @pl.when(lax.rem(rel, 2) == 1)
+        def _():
+            reduce_copy(part, place, 2).wait_send()
+            reduce_copy(part, place, 3).wait_send()
+
+    def z_copy(place):
+        dz, dy = place
+        return pltpu.make_async_remote_copy(
+            src_ref=D.at[dz, dy, pl.ds(0, z_rows)], dst_ref=RZ.at[dy],
+            send_sem=sz.at[dy], recv_sem=rz.at[dy], device_id=Z2, device_id_type=MESH)
+
+    def early_send(k):
+        if not z_rows:
+            return
+
+        @pl.when(owner_z(ORDER[k]) != zh)
+        def _():
+            z_copy(ORDER[k]).start()
+
+    def early_first(k):
+        if not z_rows:
+            return
+        place = ORDER[k]
+        dz, dy = place
+
+        @pl.when(owner_z(place) == zh)
+        def _():
+            z_copy(place).wait_recv()
+            span = pl.ds(0, z_rows)
+            D[dz, dy, span, :] = (D[dz, dy, span, :].astype(F32) + RZ[dy].astype(F32)).astype(BF16)
+            reduce_first(early, place)
+
+    def early_relay(k):
+        if not z_rows:
+            return
+        @pl.when(owner_z(ORDER[k]) == zh)
+        def _():
+            reduce_relay(early, ORDER[k])
+
+    def relay(k):
+        reduce_relay(late, ORDER[k])
 
     def slice_work(k):
         place = ORDER[k]
@@ -302,37 +425,36 @@
         lax.fori_loop(0, nb, step, 0)
         if k + 2 < len(ORDER):
             down_load(k + 2).start()
-        rel = relation(place)
-
-        @pl.when(rel == 2)
-        def _():
-            reduce_copy(place, 0).start()
-            reduce_copy(place, 1).start()
-
-        @pl.when(lax.rem(rel, 2) == 1)
-        def _():
-            reduce_copy(place, 2).start()
-
-    def relay(k):
-        place = ORDER[k]
-        dz, dy = place
-        rel = relation(place)
-        zz = owner_z(place)
-        side = rel // 2
-
-        @pl.when(lax.rem(rel, 2) == 1)
-        def _():
-            pltpu.make_async_remote_copy(
-                src_ref=D.at[dz, dy, pl.ds(0, half_u)], dst_ref=R1.at[zz, side],
-                send_sem=s1.at[zz, side], recv_sem=r1.at[zz, side],
-                device_id=Xp, device_id_type=MESH).wait_recv()
-            span = rows(side * half_u, half_u)
-            D[dz, dy, span, :] = (D[dz, dy, span, :].astype(F32) + R1[zz, side].astype(F32)).astype(BF16)
-            reduce_copy(place, 3).start()
+        if k < 7:
+            reduce_first(late, place)
+
+    def row_loads(n, slot):
+        core = jnp.where(n < 8, 1 - c, c)
+        at = rows((2 * lax.rem(n, 8) + core) * 256, 256)
+        return (
+            pltpu.make_async_copy(wg.at[at, :], wrow.at[slot, :, cols(0, units)], ls.at[16 + 2 * slot]),
+            pltpu.make_async_copy(wu.at[at, :], wrow.at[slot, :, cols(units, units)], ls.at[17 + 2 * slot]),
+        )
+
+    def input_part(first):
+        def step(n, _):
+            slot = lax.rem(n, 2)
+            for cp in row_loads(n, slot):
+                cp.wait()
+            X[:, cols(n * 256, 256)] = dot_nt(G[0:tok, :], wrow[slot]).astype(BF16)
+
+            @pl.when(n + 2 < 16)
+            def _():
+                for cp in row_loads(n + 2, slot):
+                    cp.start()
+            return 0
+
+        lax.fori_loop(first, first + 4, step, 0)
 
     gl.along_z()
     gl.got("C", (0, 0))
     slice_work(0)
+    xt_along_z()
     gl.neighbours0()
     gl.got("C", (1, 0))
     slice_work(1)
@@ -341,25 +463,30 @@
     gl.got("C", (0, 1))
     slice_work(3)
     gl.opposite0()
-    for k, cp in x_moves:
-        cp.wait_recv()
-        piece = XT.at[c, :, cols(k * tok, tok)]
-        xt_c.append(send(piece, piece, C))
+    for k in range(4):
+        early_send(k)
     relay(0)
     gl.got("C", (0, 2))
     slice_work(4)
+    early_send(4)
     gl.neighbours1()
+    xt_around_y()
     relay(1)
     gl.got("C", (1, 3))
     slice_work(5)
+    early_send(5)
     gl.got("C", (1, 1))
     slice_work(6)
+    early_send(6)
     gl.opposite1()
     relay(2)
     relay(3)
+    for slot in range(2):
+        for cp in row_loads(slot, slot):
+            cp.start()
     gl.got("C", (1, 2))
     slice_work(7)
-    relay(4)
+    early_send(7)
 
     def grads(b, _):
         at = cols(b * BLOCK, BLOCK)
@@ -406,68 +533,53 @@
                 lane = j * 256 + i * BLOCK
                 target, lane = (o_g, lane) if lane < units else (o_u, lane - units)
                 target[r, lane:lane + BLOCK] = out[:, i * BLOCK:(i + 1) * BLOCK]
-
-    def row_loads(i, slot, core):
-        at = rows((2 * i + core) * 256, 256)
-        return (
-            pltpu.make_async_copy(wg.at[at, :], wrow.at[slot, :, cols(0, units)], ls.at[16 + 2 * slot]),
-            pltpu.make_async_copy(wu.at[at, :], wrow.at[slot, :, cols(units, units)], ls.at[17 + 2 * slot]),
-        )
-
-    def input_part(core, offset):
-        def step(i, _):
-            slot = lax.rem(i, 2)
-            for cp in row_loads(i, slot, core):
-                cp.wait()
-            X[:, cols(offset + i * 256, 256)] = dot_nt(G[0:tok, :], wrow[slot]).astype(BF16)
-
-            @pl.when(i + 2 < 8)
-            def _():
-                for cp in row_loads(i + 2, slot, core):
-                    cp.start()
-            return 0
-
-        for slot in range(2):
-            for cp in row_loads(slot, slot, core):
-                cp.start()
-        lax.fori_loop(0, 8, step, 0)
-
-    def sum_x(zz):
+        for i in range(2):
+            lane = j * 256 + i * BLOCK
+            held, out, lane = (o_g, to_g, lane) if lane < units else (o_u, to_u, lane - units)
+            store(held.at[:, cols(lane, BLOCK)], out.at[:, cols(lane, BLOCK)])
+
+    def sum_x(part, zz):
+        base, half, one, two, send1, recv1, send2, recv2 = part
         for side in range(2):
             for i in range(2):
-                span = pl.ds(0, half_u)
                 pltpu.make_async_remote_copy(
-                    src_ref=D.at[0, 0, span], dst_ref=R2.at[zz, side, span],
-                    send_sem=s2.at[zz, side, i], recv_sem=r2.at[zz, side, i],
+                    src_ref=D.at[0, 0, pl.ds(base, half)],
+                    dst_ref=at_owner(two, part, zz, side, pl.ds(0, half)),
+                    send_sem=at_owner(send2, part, zz, side, i), recv_sem=at_owner(recv2, part, zz, side, i),
                     device_id=Xp, device_id_type=MESH).wait_recv()
-        return down_place(zz)
 
     def down_place(zz):
         return zl + zz - 2 * zl * zz, lax.rem(x - y + 4, 4)
 
     down_z = []
 
-    def down_away(half):
+    def down_away():
         zz = 1 - zh
-        dz, dy = sum_x(zz) if half == 0 else down_place(zz)
-        at = pl.ds(half * half_u, half_u)
-        D[dz, dy, at, :] = (D[dz, dy, at, :].astype(F32) + R2[zz, 0, at, :].astype(F32)
-                            + R2[zz, 1, at, :].astype(F32)).astype(BF16)
-        down_z.append(send(D.at[dz, dy, at], R3.at[at], Z2))
+        sum_x(late, zz)
+        dz, dy = down_place(zz)
+        at = pl.ds(z_rows, units - z_rows)
+        D[dz, dy, at, :] = (D[dz, dy, at, :].astype(F32) + R2[zz, 0].astype(F32)
+                            + R2[zz, 1].astype(F32)).astype(BF16)
+        down_z.append(send(D.at[dz, dy, at], R3.at[...], Z2))
+
+    def down_own_early():
+        if not z_rows:
+            return
+        sum_x(early, zh)
+        dz, dy = down_place(zh)
+        at = pl.ds(0, z_rows)
+        o_d[at, :] = (D[dz, dy, at, :].astype(F32) + R2A[0].astype(F32) + R2A[1].astype(F32)).astype(BF16)
+        store(o_d.at[at], to_d.at[at])
 
     def down_own():
-        zz = zh
-        dz, dy = sum_x(zz)
+        sum_x(late, zh)
         for cp in down_z:
             cp.wait_recv()
-
-        def step(b, _):
-            at = rows(b * BLOCK, BLOCK)
-            o_d[at, :] = (D[dz, dy, at, :].astype(F32) + R2[zz, 0, at, :].astype(F32)
-                          + R2[zz, 1, at, :].astype(F32) + R3[at, :].astype(F32)).astype(BF16)
-            return 0
-
-        lax.fori_loop(0, nb, step, 0)
+        dz, dy = down_place(zh)
+        at = pl.ds(z_rows, units - z_rows)
+        o_d[at, :] = (D[dz, dy, at, :].astype(F32) + R2[zh, 0].astype(F32) + R2[zh, 1].astype(F32)
+                      + R3[...].astype(F32)).astype(BF16)
+        store(o_d.at[at], to_d.at[at])
 
     in_y, in_z = [], []
 
@@ -495,41 +607,61 @@
     def input_sum_z():
         in_z[0].wait_recv()
         o_in[...] = (X[:, cols(2048 + zl * 1024 + y * 256, 256)].astype(F32) + IrZ[...].astype(F32)).astype(BF16)
+        store(o_in, to_in)
 
     g_own(0)
     g_own(1)
-    g_own(2)
+    reduce_first(late, ORDER[7])
     for cp in x_sends:
         cp.wait_send()
-    input_part(1 - c, 0)
+    input_part(0)
+    relay(4)
+    relay(5)
+    g_forward(0)
+    g_own(2)
+    input_part(4)
     in_c = send(X.at[:, cols(0, 2048)], IrC.at[...], C)
-    relay(5)
+    xt_cores()
     relay(6)
-    input_part(c, 2048)
+    g_forward(1)
+    g_own(3)
+    early_first(0)
+    early_first(1)
+    xt_moves["C"].wait_recv()
+    p_other(0)
+    input_part(8)
+    g_forward(2)
+    g_own(4)
+    p_other(1)
+    input_part(12)
+    input_sum_cores()
     relay(7)
-    for cp in xt_c:
-        cp.wait_recv()
-    input_sum_cores()
-    g_forward(0)
-    g_own(3)
-    g_forward(1)
-    g_own(4)
-    down_away(0)
-    down_away(1)
-    p_other(0)
-    g_forward(2)
+    early_first(2)
+    early_first(3)
+    early_relay(0)
+    early_relay(1)
+    g_forward(3)
     g_own(5)
-    p_other(1)
-    g_forward(3)
+    p_other(2)
+    early_first(4)
+    early_first(5)
+    early_first(6)
+    early_first(7)
+    early_relay(2)
+    early_relay(3)
+    g_forward(4)
     g_own(6)
-    p_other(2)
-    input_sum_y()
-    g_forward(4)
     p_other(3)
+    p_own(0)
+    early_relay(4)
+    early_relay(5)
+    early_relay(6)
+    early_relay(7)
     g_forward(5)
-    p_own(0)
+    down_away()
     p_other(4)
     p_own(1)
+    input_sum_y()
     g_forward(6)
     p_other(5)
     p_own(2)
@@ -537,25 +669,28 @@
     input_sum_z()
     p_own(3)
     p_own(4)
+    down_own_early()
+    p_own(5)
     down_own()
-    p_own(5)
     p_own(6)
 
+    for cp in stored:
+        cp.wait()
     for cp in started:
         if not any(cp is other for other in x_sends):
             cp.wait_send()
     for place in ORDER:
-        rel = relation(place)
-
-        @pl.when(rel == 2)
-        def _():
-            reduce_copy(place, 0).wait_send()
-            reduce_copy(place, 1).wait_send()
-
-        @pl.when(lax.rem(rel, 2) == 1)
-        def _():
-            reduce_copy(place, 2).wait_send()
-            reduce_copy(place, 3).wait_send()
+        reduce_drain(late, place)
+        if not z_rows:
+            continue
+
+        @pl.when(owner_z(place) == zh)
+        def _():
+            reduce_drain(early, place)
+
+        @pl.when(owner_z(place) != zh)
+        def _():
+            z_copy(place).wait_send()
 
 
 def hand_out(*refs):
@@ -576,8 +711,9 @@
     width, units = w_gate.shape
     anywhere = pl.BlockSpec(memory_space=pl.ANY)
     smem = pl.BlockSpec(memory_space=pltpu.SMEM)
-    vmem = pl.BlockSpec(memory_space=pltpu.VMEM)
     share = width // 8
+    z_rows = Z_BLOCKS * BLOCK
+    held = max(z_rows, 32)
     V = pltpu.VMEM
     dma = pltpu.SemaphoreType.DMA
     scratch = [V((2, LEVELS, tok, 256), BF16) for _ in ORDER] + [
@@ -585,13 +721,13 @@
         V((4, width // 2, 256), BF16),
         V((2, units, 512), BF16),
         V((2, 256, 2 * units), BF16),
-        V((3, 512, tok), BF16),
+        V((3, 64, tok), BF16),
         V((2, 512, 4 * tok), BF16),
         V((4 * tok, 2 * units), BF16),
         V((2, 4, units, 512), BF16),
-        V((2, 2, units // 2, 512), BF16),
-        V((2, 2, units, 512), BF16),
-        V((units, 512), BF16),
+        V((2, 2, (units - z_rows) // 2, 512), BF16),
+        V((2, 2, units - z_rows, 512), BF16),
+        V((units - z_rows, 512), BF16),
         V((7, 512, 256), BF16),
         V((7, 512, 256), BF16),
         V((tok, width // 2), BF16),
@@ -608,9 +744,23 @@
         dma((2, 2)),
         dma((2, 2, 2)),
         dma((2, 2, 2)),
+        V((4, held, 512), BF16),
+        V((2, held // 2, 512), BF16),
+        V((2, held, 512), BF16),
+        dma((2,)),
+        dma((2,)),
+        dma((2, 2)),
+        dma((2, 2)),
+        dma((4,)),
+        dma((4,)),
+        V((tok, 256), BF16),
+        V((share, units), BF16),
+        V((share, units), BF16),
+        V((units, share), BF16),
+        dma((24,)),
     ]
     results = pl.pallas_call(
-        functools.partial(body, tok, width, units),
+        functools.partial(body, tok, width, units, z_rows),
         out_shape=(
             jax.ShapeDtypeStruct((tok, 256), BF16),
             jax.ShapeDtypeStruct((share, units), BF16),
@@ -618,7 +768,7 @@
             jax.ShapeDtypeStruct((units, share), BF16),
         ),
         in_specs=[smem, smem] + [anywhere] * 5,
-        out_specs=(vmem,) * 4,
+        out_specs=(anywhere,) * 4,
         scratch_shapes=scratch,
         compiler_params=pltpu.CompilerParams(
             collective_id=0, has_side_effects=True, vmem_limit_bytes=64 * 2**20),

time: 198 us -> 172 us (0.87); the launches traced: 194 us -> 171 us
  Pallas kernels: 193 us -> 170 us
    pallas_call x1, Pallas kernels: 191 us -> 167 us  [on_device(): pl.pallas_call(functools.partial(body, tok, width, units, z_rows), out_sh...]
where the time goes in v3:
time: 172 us; the launch traced here: 171 us
  Pallas kernels  170 us (99%)
    pallas_call x1, Pallas kernels, on_device(): pl.pallas_call(functools.partial(body, tok, width, units, z_rows), out_sh...  167 us

profile of v3, /device:TPU:4, one launch (start us, length us, event | category | flops | bytes accessed | tf_op | source)
XLA Modules:
  0.0 171.0 jit_solution(14101893061355746280)
XLA Ops:
  0.6 167.3 %swiglu_backward.1 = (bf16[384,256]{1,0:T(8,128)(2,1)}, bf16[512,896]{1,0:T(8,128)(2,1)}, bf16[512,896]{1,0:T(8,128)(2,1)}, bf16[896,512]{1,0:T(8,128)(2,1)}) custom-call(s32[4]{0:T(128)} %refs_0_.1, s32[7]{0:T(128)} %refs_1_.1, bf16[384,256]{1,0:T(8,128)(2,1)} %refs_2_.1, bf16[4096,896]{1,0:T(8,128)(2,1)} %refs_3_.1, bf16[4096,896]{1,0:T(8,128)(2,1)} %refs_4_.1, ...), custom_call_target="tpu_custom_call" | custom-call | tf_op jit(solution)/shard_map/swiglu_backward/pallas_call | solution.py:762
  167.9 2.9 %hand_out.1 = (bf16[384,256]{1,0:T(8,128)(2,1)}, bf16[512,896]{1,0:T(8,128)(2,1)}, bf16[512,896]{1,0:T(8,128)(2,1)}, bf16[896,512]{1,0:T(8,128)(2,1)}) custom-call(bf16[384,256]{1,0:T(8,128)(2,1)} %get-tuple-element.8.refs_0_, bf16[512,896]{1,0:T(8,128)(2,1)} %get-tuple-element.9.refs_1_, bf16[512,896]{1,0:T(8,128)(2,1)} %get-tuple-element.10.refs_2_, ...), custom_call_target="tpu_custom_call" | custom-call | tf_op jit(solution)/shard_map/hand_out/pallas_call | solution.py:777

commit v4 on v3

--- a/solution.py
+++ b/solution.py
@@ -137,7 +137,7 @@
         def send(self, step, place, first=0, count=4, src=None):
             dz, dy = place
             moved, dev = {"C": (place, C), "Z": ((1 - dz, dy), Z1), "P": ((dz, (dy + 3) % 4), Yp),
-                          "M": ((dz, (dy + 1) % 4), Ym)}[step]
+                          "M": ((dz, (dy + 1) % 4), Ym)}[step[0]]
             mine, there = self.pair(place, moved, first, count)
             self.moves[step, place] = send(mine if src is None else src, there, dev)
 
@@ -158,20 +158,30 @@
             self.send("M", (1, 0), 0, self.cut)
             self.send("C", (1, 0))
 
+        def neighbours0_late(self):
+            self.got("P2", (0, 0))
+            self.late_z((0, 3))
+            self.got("M2", (0, 0))
+            self.send("M", (0, 1), 2, 2)
+            self.late_z((0, 1))
+
         def neighbours0(self):
             self.got("P", (0, 0))
             self.send("P", (0, 3), 0, 2)
-            self.late_z((0, 3))
             self.send("C", (0, 3))
             self.got("M", (0, 0))
-            self.send("M", (0, 1), 2, 2)
-            self.late_z((0, 1))
+            if self.cut == 4:
+                self.send("M", (0, 1), 2, 2)
             self.send("C", (0, 1))
+
+        def opposite0_late(self):
+            self.got("M", (0, 1))
+            self.late_z((0, 2))
 
         def opposite0(self):
             self.got("P", (0, 3))
-            self.got("M", (0, 1))
-            self.late_z((0, 2))
+            if self.cut == 4:
+                self.got("M", (0, 1))
             self.send("C", (0, 2))
 
         def neighbours1(self):
@@ -209,8 +219,10 @@
     gx.neighbours0()
     gx.opposite0()
     gx.neighbours1()
-    gl.send("P", (0, 0))
-    gl.send("M", (0, 0))
+    gl.send("P2", (0, 0), 2, 2)
+    gl.send("M2", (0, 0), 2, 2)
+    gl.send("P", (0, 0), 0, 2)
+    gl.send("M", (0, 0), 0, 2)
     own_x.wait()
     for dy in range(4):
         gx.got("C", (0, dy))
@@ -451,34 +463,36 @@
 
         lax.fori_loop(first, first + 4, step, 0)
 
+    gl.neighbours0_late()
     gl.along_z()
     gl.got("C", (0, 0))
     slice_work(0)
     xt_along_z()
-    gl.neighbours0()
     gl.got("C", (1, 0))
     slice_work(1)
+    gl.neighbours0()
     gl.got("C", (0, 3))
     slice_work(2)
     gl.got("C", (0, 1))
     slice_work(3)
-    gl.opposite0()
+    gl.opposite0_late()
     for k in range(4):
         early_send(k)
     relay(0)
+    gl.opposite0()
+    gl.neighbours1()
     gl.got("C", (0, 2))
     slice_work(4)
     early_send(4)
-    gl.neighbours1()
     xt_around_y()
     relay(1)
     gl.got("C", (1, 3))
     slice_work(5)
     early_send(5)
+    gl.opposite1()
     gl.got("C", (1, 1))
     slice_work(6)
     early_send(6)
-    gl.opposite1()
     relay(2)
     relay(3)
     for slot in range(2):
@@ -627,13 +641,13 @@
     g_own(3)
     early_first(0)
     early_first(1)
+    input_part(8)
     xt_moves["C"].wait_recv()
     p_other(0)
-    input_part(8)
     g_forward(2)
     g_own(4)
+    input_part(12)
     p_other(1)
-    input_part(12)
     input_sum_cores()
     relay(7)
     early_first(2)
@@ -652,6 +666,7 @@
     g_forward(4)
     g_own(6)
     p_other(3)
+    input_sum_y()
     p_own(0)
     early_relay(4)
     early_relay(5)
@@ -661,19 +676,19 @@
     down_away()
     p_other(4)
     p_own(1)
-    input_sum_y()
     g_forward(6)
     p_other(5)
     p_own(2)
     p_other(6)
-    input_sum_z()
     p_own(3)
     p_own(4)
     down_own_early()
     p_own(5)
+    input_sum_z()
     down_own()
     p_own(6)
 
+    assert len(started) <= COPIES and len(stored) <= 24
     for cp in stored:
         cp.wait()
     for cp in started:

time: 172 us -> 169 us (0.983)
  Pallas kernels: 170 us -> 168 us
    pallas_call x1, Pallas kernels: 167 us -> 165 us  [on_device(): pl.pallas_call(functools.partial(body, tok, width, units, z_rows), out_sh...]
where the time goes in v4:
time: 169 us; the launch traced here: 168 us
  Pallas kernels  168 us (99%)
    pallas_call x1, Pallas kernels, on_device(): pl.pallas_call(functools.partial(body, tok, width, units, z_rows), out_sh...  165 us

profile of v4, /device:TPU:4, one launch (start us, length us, event | category | flops | bytes accessed | tf_op | source)
XLA Modules:
  0.0 168.3 jit_solution(14313118681424396017)
XLA Ops:
  0.6 164.6 %swiglu_backward.1 = (bf16[384,256]{1,0:T(8,128)(2,1)}, bf16[512,896]{1,0:T(8,128)(2,1)}, bf16[512,896]{1,0:T(8,128)(2,1)}, bf16[896,512]{1,0:T(8,128)(2,1)}) custom-call(s32[4]{0:T(128)} %refs_0_.1, s32[7]{0:T(128)} %refs_1_.1, bf16[384,256]{1,0:T(8,128)(2,1)} %refs_2_.1, bf16[4096,896]{1,0:T(8,128)(2,1)} %refs_3_.1, bf16[4096,896]{1,0:T(8,128)(2,1)} %refs_4_.1, ...), custom_call_target="tpu_custom_call" | custom-call | tf_op jit(solution)/shard_map/swiglu_backward/pallas_call | solution.py:777
  165.3 2.9 %hand_out.1 = (bf16[384,256]{1,0:T(8,128)(2,1)}, bf16[512,896]{1,0:T(8,128)(2,1)}, bf16[512,896]{1,0:T(8,128)(2,1)}, bf16[896,512]{1,0:T(8,128)(2,1)}) custom-call(bf16[384,256]{1,0:T(8,128)(2,1)} %get-tuple-element.8.refs_0_, bf16[512,896]{1,0:T(8,128)(2,1)} %get-tuple-element.9.refs_1_, bf16[512,896]{1,0:T(8,128)(2,1)} %get-tuple-element.10.refs_2_, ...), custom_call_target="tpu_custom_call" | custom-call | tf_op jit(solution)/shard_map/hand_out/pallas_call | solution.py:792

commit v5 on v4

--- a/solution.py
+++ b/solution.py
@@ -710,13 +710,18 @@
 
 def hand_out(*refs):
     src, dst, held, sems = refs[:4], refs[4:8], refs[8:12], refs[12]
-    into = [pltpu.make_async_copy(src[i], held[i], sems.at[0, i]) for i in range(4)]
-    out = [pltpu.make_async_copy(held[i], dst[i], sems.at[1, i]) for i in range(4)]
+    into, out = [], []
+    for part in range(4):
+        for i in range(4):
+            size = src[i].shape[0] // 4
+            at = pl.ds(part * size, size)
+            into.append(pltpu.make_async_copy(src[i].at[at], held[i].at[at], sems.at[0, i, part]))
+            out.append(pltpu.make_async_copy(held[i].at[at], dst[i].at[at], sems.at[1, i, part]))
     for cp in into:
         cp.start()
-    for i in range(4):
-        into[i].wait()
-        out[i].start()
+    for arrived, leaving in zip(into, out):
+        arrived.wait()
+        leaving.start()
     for cp in out:
         cp.wait()
 
@@ -794,7 +799,7 @@
         out_shape=tuple(jax.ShapeDtypeStruct(r.shape, r.dtype) for r in results),
         in_specs=[anywhere] * 4,
         out_specs=(anywhere,) * 4,
-        scratch_shapes=[V(r.shape, r.dtype) for r in results] + [dma((2, 4))],
+        scratch_shapes=[V(r.shape, r.dtype) for r in results] + [dma((2, 4, 4))],
         name="hand_out",
     )(*results)
 

time: 169 us -> 169 us (level)
  no operation moved by 1% of the time
where the time goes in v5:
time: 169 us; the launch traced here: 168 us
  Pallas kernels  168 us (99%)
    pallas_call x1, Pallas kernels, on_device(): pl.pallas_call(functools.partial(body, tok, width, units, z_rows), out_sh...  165 us

profile of v5, /device:TPU:4, one launch (start us, length us, event | category | flops | bytes accessed | tf_op | source)
XLA Modules:
  0.0 168.5 jit_solution(11454103650769158635)
XLA Ops:
  0.6 164.6 %swiglu_backward.1 = (bf16[384,256]{1,0:T(8,128)(2,1)}, bf16[512,896]{1,0:T(8,128)(2,1)}, bf16[512,896]{1,0:T(8,128)(2,1)}, bf16[896,512]{1,0:T(8,128)(2,1)}) custom-call(s32[4]{0:T(128)} %refs_0_.1, s32[7]{0:T(128)} %refs_1_.1, bf16[384,256]{1,0:T(8,128)(2,1)} %refs_2_.1, bf16[4096,896]{1,0:T(8,128)(2,1)} %refs_3_.1, bf16[4096,896]{1,0:T(8,128)(2,1)} %refs_4_.1, ...), custom_call_target="tpu_custom_call" | custom-call | tf_op jit(solution)/shard_map/swiglu_backward/pallas_call | solution.py:782
  165.3 3.0 %hand_out.1 = (bf16[384,256]{1,0:T(8,128)(2,1)}, bf16[512,896]{1,0:T(8,128)(2,1)}, bf16[512,896]{1,0:T(8,128)(2,1)}, bf16[896,512]{1,0:T(8,128)(2,1)}) custom-call(bf16[384,256]{1,0:T(8,128)(2,1)} %get-tuple-element.8.refs_0_, bf16[512,896]{1,0:T(8,128)(2,1)} %get-tuple-element.9.refs_1_, bf16[512,896]{1,0:T(8,128)(2,1)} %get-tuple-element.10.refs_2_, ...), custom_call_target="tpu_custom_call" | custom-call | tf_op jit(solution)/shard_map/hand_out/pallas_call | solution.py:797
